TPU v7x, 512 devices: a whole 4x4x16 slice. The times are simulated.
512 devices in a mesh: dp: 32 (over z_lo, y), label: 16 (over z_hi, x, core).
Axes of the slice: x: 4, y: 4, z: 16 (z_hi: 2, z_lo: 8; z = z_hi * 8 + z_lo), core: 2. Of those that a mesh axis runs over, the one named last changes fastest.
Arguments:
- features: bfloat16 [4096, 768], P('dp', 'label')
- label_ids: int32 [4096, 32], P('dp'), may hold values from 0 to 131071
- label_count: int32 [4096], P('dp'), may hold values from 1 to 32
- weight: float32 [131072, 768], P(('dp', 'label'))
- moment: float32 [131072, 768], P(('dp', 'label')), may hold values from -1.9073486e-05 to 1.9073486e-05
- second: float32 [131072, 768], P(('dp', 'label')), may hold values from 1e-13 to 1e-11
Outputs:
- lamb_step: float32 [131072, 768], P(('dp', 'label'))
- new_moment: float32 [131072, 768], P(('dp', 'label'))
- new_second: float32 [131072, 768], P(('dp', 'label'))
All inputs are finite; a program needn't handle non-finite values.
Results may differ from a plain program's by a relative error of at most 0.0017.
Values may be sent and summed in bfloat16 or wider, within the bound.
A program may use at most 64 MiB of HBM per device.

v0:
```python
import jax
import jax.numpy as jnp
from jax import lax
from jax.sharding import PartitionSpec as P

STEP = 10


def grad_piece(queries, slot_ids, slot_count, weight_bf, first_row, scale, inv_total):
    rows_here = weight_bf.shape[0]
    scores = (
        lax.dot_general(
            queries, weight_bf, (((1,), (1,)), ((), ())), preferred_element_type=jnp.float32
        )
        * scale
    )
    slot_ok = lax.iota(jnp.int32, slot_ids.shape[1])[None, :] < slot_count[:, None]
    local = jnp.where(slot_ok, slot_ids - first_row, -1).astype(jnp.int32)
    columns = lax.iota(jnp.int32, rows_here)
    targets = jnp.any(local[:, :, None] == columns[None, None, :], axis=1).astype(jnp.float32)
    dscore = ((jax.nn.sigmoid(scores) - targets) * inv_total).astype(jnp.bfloat16)
    return (
        lax.dot_general(
            dscore, queries, (((0,), (0,)), ((), ())), preferred_element_type=jnp.float32
        )
        * scale
    )


def shards(features, label_ids, label_count, weight, moment, second):
    rows_here = weight.shape[0]
    n_label = lax.axis_size("label")
    width = features.shape[1] * n_label
    total = features.shape[0] * lax.axis_size("dp")
    scale = 1.0 / width**0.5
    inv_total = 1.0 / total
    first_row = (lax.axis_index("dp") * n_label + lax.axis_index("label")) * rows_here
    weight_bf = weight.astype(jnp.bfloat16)
    wide = lax.all_gather(features, "label", axis=1, tiled=True)
    grad = grad_piece(
        lax.all_gather(wide, "dp", axis=0, tiled=True),
        lax.all_gather(label_ids, "dp", axis=0, tiled=True),
        lax.all_gather(label_count, "dp", axis=0, tiled=True),
        weight_bf,
        first_row,
        scale,
        inv_total,
    )
    new_moment = 0.9 * moment + 0.1 * grad
    new_second = 0.999 * second + 0.001 * grad * grad
    update = (
        new_moment / (1.0 - 0.9**STEP) / (jnp.sqrt(new_second / (1.0 - 0.999**STEP)) + 1e-06)
        + 0.01 * weight
    )
    weight_sq, update_sq = lax.psum(
        (jnp.sum(weight * weight), jnp.sum(update * update)), ("dp", "label")
    )
    trust = jnp.sqrt(weight_sq) / (jnp.sqrt(update_sq) + 1e-06)
    return (trust * update, new_moment, new_second)


def solution(mesh):
    in_specs = (
        P("dp", "label"),
        P("dp", None),
        P("dp"),
        P(("dp", "label"), None),
        P(("dp", "label"), None),
        P(("dp", "label"), None),
    )
    out_specs = (P(("dp", "label"), None), P(("dp", "label"), None), P(("dp", "label"), None))
    return jax.shard_map(shards, mesh=mesh, in_specs=in_specs, out_specs=out_specs, check_vma=False)
```

profile of v0, /device:TPU:1, one launch (start us, length us, event | category | flops | bytes accessed | tf_op | source)
XLA Modules:
  0.0 440.9 jit_solution(11140272909285514778)
XLA Ops:
  7.2 0.0 all-gather.3.cloned.1.call-start
  7.2 52.9 %all_gather.12 = bf16[128,768]{0,1:T(8,128)(2,1)} all-gather(bf16[128,48]{0,1:T(8,128)(2,1)} %param.6), channel_id=1, replica_groups=mesh['dp'=32,'label'=16] {'label'}, dimensions={1}, use_global_device_ids=true | all-gather | bytes 208896 | tf_op jit(solution)/shard_map/all_gather | solution.py:39
  60.1 0.0 all-gather.3.cloned.1.call-update
  60.1 104.5 %all-gather = s32[32,1,128]{2,1,0:T(1,128)S(1)} all-gather(s32[1,1,128]{2,1,0:T(1,128)} %bitcast.5), channel_id=1, replica_groups=mesh['dp'=32,'label'=16] {'dp'}, dimensions={0}, use_global_device_ids=true | all-gather | bytes 16896 | tf_op jit(solution)/shard_map/all_gather | solution.py:43
  164.6 101.5 %all_gather.15 = s32[4096,32]{0,1:T(8,128)S(1)} all-gather(s32[128,32]{0,1:T(8,128)} %param.7), channel_id=1, replica_groups=mesh['dp'=32,'label'=16] {'dp'}, dimensions={0}, use_global_device_ids=true | all-gather | bytes 540672 | tf_op jit(solution)/shard_map/all_gather | solution.py:42
  266.2 0.1 subtract_select_fusion
  266.2 0.6 copy.11
  266.8 25.9 %fusion = pred[4096,256]{1,0:T(8,128)(4,1)S(1)} fusion(s32[4096,32]{1,0:T(8,128)S(1)} %copy.11), kind=kLoop, calls=%fused_computation.1 | loop fusion | flops 66060288 | bytes 1572864 | tf_op jit(solution)/shard_map/reduce_or | solution.py:20
  292.8 0.0 all-gather.3.cloned.1.call-done
  292.8 14.3 %multiply_reduce_fusion = (f32[]{:T(128)}, f32[256,768]{1,0:T(8,128)S(1)}, f32[256,768]{1,0:T(8,128)}, f32[256,768]{1,0:T(8,128)}, f32[]{:T(128)}) fusion(f32[256,768]{1,0:T(8,128)} %param.9, f32[256,768]{1,0:T(8,128)} %param.10, f32[256,768]{1,0:T(8,128)} %param.11, bf16[4096,768]{0,1:T(8,128)(2,1)} %all-gather.3.cloned.1.call-done, ...), kind=kOutput, calls=%fused_computation.11 | convolution fusion | flops 3233349632 | bytes 12058632 | tf_op jit(solution)/shard_map/dot_general | solution.py:23
  307.1 124.6 %all-reduce = (f32[]{:T(128)}, f32[]{:T(128)}) all-reduce(f32[]{:T(128)} %get-tuple-element.9, f32[]{:T(128)} %get-tuple-element.5), channel_id=1, replica_groups=mesh['dp'=32,'label'=16] {'dp','label'}, use_global_device_ids=true, to_apply=%region_1.2 | all-reduce | flops 2 | bytes 16 | tf_op jit(solution)/shard_map/psum | solution.py:55
  433.1 0.9 broadcast_multiply_fusion
Async XLA Ops:
  7.2 285.6 %all-gather.3.cloned.1.call-start = ((), (), s32[]{:S(2)}) async-start(), calls=%async_computation | async-start | bytes 6488064 | tf_op jit(solution)/shard_map/all_gather | solution.py:41
Sparse Core Ops, SparseCore 0:
  60.2 179.5 all-gather.2
where the time goes:
time: 441 us
  blocking collectives  383 us (87%)
  other arithmetic  26.9 us (6%)
  between operations  15.5 us (4%)
  matrix products  14.3 us (3%)
    psum x1, blocking collectives, shards(): lax.psum((jnp.sum(weight * weight), jnp.sum(update * update)), ('dp', 'la...  125 us
    all_gather x1, blocking collectives, shards(): lax.all_gather(label_count, 'dp', axis=0, tiled=True)  104 us
    all_gather x1, blocking collectives, shards(): lax.all_gather(label_ids, 'dp', axis=0, tiled=True)  102 us
    all_gather x1, blocking collectives, shards(): wide = lax.all_gather(features, 'label', axis=1, tiled=True)  52.9 us
    reduce_or x1, other arithmetic, grad_piece(): jnp.any(local[:, :, None] == columns[None, None, :], axis=1)  25.9 us
    dot_general x1, matrix products, grad_piece(): lax.dot_general(dscore, queries, (((0,), (0,)), ((), ())), preferred_elem...  14.3 us
  transfers between devices with their start and end apart: 1, of which 0 were waited for; matrix products, arithmetic and copies ran while one was open for 6% of the time, Pallas kernels for 0%

commit v1 on v0

v1 whole, which is shorter than its diff:
```python
import functools

import jax
import jax.numpy as jnp
from jax import lax
from jax.experimental import pallas as pl
from jax.experimental.pallas import tpu as pltpu
from jax.sharding import PartitionSpec as P

STEP = 10
MESH = pl.DeviceIdType.MESH
NX, NY, NZ = 4, 4, 16
WIDTH, ROWS, QUERIES = 768, 256, 4096
HALF = WIDTH // 2
BLOCK_D, BLOCK_Q = 48, 128
SCALE = 1.0 / WIDTH**0.5

GROUPS = {
    "own": (0, 1, "y"),
    "near_up": (1, 4, "x"),
    "near_down": (13, 16, "y"),
    "mid_up": (4, 7, "x"),
    "mid_down": (10, 13, "y"),
    "far_up": (7, 9, "x"),
    "far_down": (9, 10, "y"),
}


class Sems:
    def __init__(self, send, recv):
        self.send, self.recv, self.used = send, recv, 0

    def next(self):
        self.used += 1
        return self.send.at[self.used - 1], self.recv.at[self.used - 1]


N_SEMS = 180


def kernel(
    features, ids, count, weight, moment, second,
    update_out, moment_out, second_out, trust_out,
    feat_in, ids_in, ids_t, w_in, mom_in, sec_in, w_bf, held, labels, words, acc, sums,
    send, recv, local,
):
    dp, lb = lax.axis_index("dp"), lax.axis_index("label")
    x, y, core = lax.rem(lb // 2, NX), lax.rem(dp, NY), lax.rem(lb, 2)
    z = (lb // 8) * 8 + dp // NY

    def device(x, y, z, core):
        return {"dp": lax.rem(z, 8) * NY + y, "label": (z // 8) * 8 + x * 2 + core}

    def along(axis, by):
        if axis == "x":
            return device(lax.rem(x + by, NX), y, z, core)
        if axis == "y":
            return device(x, lax.rem(y + by, NY), z, core)
        if axis == "z":
            return device(x, y, lax.rem(z + by + NZ, NZ), core)
        return device(x, y, z, 1 - core)

    barrier = pltpu.get_barrier_semaphore()
    partners = [("x", i) for i in range(1, NX)] + [("y", i) for i in range(1, NY)]
    partners += [("z", i) for i in range(1, NZ)] + [("core", 1)]
    for axis, by in partners:
        pl.semaphore_signal(barrier, inc=1, device_id=along(axis, by), device_id_type=MESH)

    loads = []
    for i, (src, dst) in enumerate(
        [(features, feat_in), (ids, ids_in), (weight, w_in), (moment, mom_in), (second, sec_in)]
    ):
        loads.append(pltpu.make_async_copy(src, dst, local.at[i]))
        loads[-1].start()

    loads[0].wait()
    held[0, y, x, core] = jnp.transpose(feat_in[...].astype(jnp.float32)).astype(jnp.bfloat16)
    loads[1].wait()
    slots = jnp.transpose(ids_in[...])
    used = lax.broadcasted_iota(jnp.int32, slots.shape, 0) < count[...]
    ids_t[...] = jnp.where(used, slots, -1).reshape(4, 8, BLOCK_Q)
    labels[3, y, x] = ids_t[x]

    sems = Sems(send, recv)
    sent = []

    def copy(src, dst, to, pair=None):
        pair = sems.next() if pair is None else pair
        c = pltpu.make_async_remote_copy(src, dst, *pair, device_id=to, device_id_type=MESH)
        sent.append(c)
        c.start()
        return c

    pl.semaphore_wait(barrier, len(partners))

    z_recv = {name: sems.next()[1] for name in GROUPS if name != "own"}
    for d in [1, 15, 2, 14, 3, 13, 4, 12, 5, 11, 6, 10, 7, 9, 8]:
        there = NZ - d
        name = next(n for n, (a, b, _) in GROUPS.items() if a <= there < b)
        copy(
            held.at[0, y, x, core], held.at[there, y, x, core], along("z", d),
            (sems.next()[0], z_recv[name]),
        )

    toward = 1 - 2 * core
    label_recv = sems.next()[1]
    for k in range(4):
        to = device(x, y, lax.rem(z + toward * (k + 1) + NZ, NZ), core)
        there = 4 if k == 3 else (2 - k) * (1 - core) + (5 + k) * core
        copy(labels.at[3, y, x], labels.at[there, y, x], to, (sems.next()[0], label_recv))

    def wait_z(name):
        a, b, _ = GROUPS[name]
        part = held.at[a:b, y, x, core]
        pltpu.make_async_remote_copy(
            part, part, send.at[0], z_recv[name], device_id=along("z", 1), device_id_type=MESH
        ).wait_recv()

    first_hop, second_hop, cross = {}, {}, {}

    def hop1(name):
        a, b, axis = GROUPS[name]
        if name != "own":
            wait_z(name)
        part = held.at[a:b, y, x, core]
        first_hop[name] = [copy(part, part, along(axis, i)) for i in (1, 3, 2)]

    def line(name, at):
        a, b, axis = GROUPS[name]
        if axis == "x":
            return held.at[a:b, at, :, core]
        return held.at[a:b, :, at, core]

    def hop2(name):
        axis = GROUPS[name][2]
        other, mine, n = ("y", y, NY) if axis == "x" else ("x", x, NX)
        for c in first_hop[name]:
            c.wait_recv()
        part = line(name, mine)
        second_hop[name] = [copy(part, part, along(other, i)) for i in (1, 3, 2)]
        cross[name] = [copy(part, part, along("core", 1))]

    def hop3(name):
        axis = GROUPS[name][2]
        mine, n = (y, NY) if axis == "x" else (x, NX)
        for c, i in zip(second_hop[name], (1, 3, 2), strict=True):
            c.wait_recv()
            part = line(name, lax.rem(mine - i + n, n))
            cross[name].append(copy(part, part, along("core", 1)))

    def done(name):
        for c in cross[name]:
            c.wait_recv()

    hop1("own")
    loads[2].wait()
    w_bf[0] = w_in[:, :HALF].astype(jnp.bfloat16)
    w_bf[1] = w_in[:, HALF:].astype(jnp.bfloat16)
    acc[...] = jnp.zeros_like(acc)

    hop1("near_up")
    hop1("near_down")
    hop2("own")
    part = labels.at[pl.ds(3 * core, 5), y, x]
    everything = labels.at[0:4, y, x]
    pltpu.make_async_remote_copy(
        everything, everything, send.at[0], label_recv, device_id=along("z", 1), device_id_type=MESH
    ).wait_recv()
    label_x = [copy(part, part, along("x", i)) for i in (1, 3, 2)]
    hop1("mid_up")
    hop1("mid_down")
    hop2("near_up")
    hop2("near_down")
    for c in label_x:
        c.wait_recv()
    part = labels.at[pl.ds(3 * core, 5), y]
    label_y = [copy(part, part, along("y", i)) for i in (1, 3, 2)]
    hop3("own")
    hop1("far_up")
    hop1("far_down")
    hop2("mid_up")
    hop2("mid_down")
    for c in label_y:
        c.wait_recv()
    part = labels.at[pl.ds(5 * core, 3)]
    label_core = copy(part, part, along("core", 1))
    hop3("near_up")
    hop3("near_down")
    hop2("far_up")
    hop2("far_down")

    label_core.wait_recv()
    first = (dp * 16 + lb) * ROWS

    def mark(i, _):
        pos, at = i // NY, lax.rem(i, NY)
        pair = jnp.where(pos < 3, pos + 5, jnp.where(pos == 3, 0, jnp.where(pos == 4, 4, pos - 4)))
        local_id = labels[pos, at] - first
        word = local_id >> 5
        bit = jnp.left_shift(jnp.int32(1), local_id & 31)
        rows = lax.broadcasted_iota(jnp.int32, (8, BLOCK_Q), 0)
        out = jnp.zeros((8, BLOCK_Q), jnp.int32)
        for w in range(8):
            hit = jnp.where(word == w, bit, 0)
            hit = (hit[0] | hit[1]) | (hit[2] | hit[3])
            for by in (4, 2, 1):
                hit = hit | pltpu.roll(hit, by, 0)
            out = jnp.where(rows == w, hit, out)
        words[pair, at] = out
        return 0

    lax.fori_loop(0, 8 * NY, mark, 0)

    def pair(r, _):
        r = lax.rem(r, 8)
        lo = lax.rem(z + r, NZ) // 8
        q = NY * BLOCK_Q

        def slab(at):
            return jnp.concatenate([held[at, i].reshape(HALF, BLOCK_Q) for i in range(NY)], axis=1)

        near, far = slab(r), slab(r + 8)
        scores = jnp.dot(w_bf[lo], near, preferred_element_type=jnp.float32)
        scores += jnp.dot(w_bf[1 - lo], far, preferred_element_type=jnp.float32)
        prob = jax.nn.sigmoid(scores * SCALE)
        marks = jnp.concatenate([words[r, i] for i in range(NY)], axis=1)
        rows = lax.broadcasted_iota(jnp.int32, (32, q), 0)
        bits = jnp.left_shift(jnp.int32(1), rows)
        target = jnp.concatenate(
            [(jnp.broadcast_to(marks[w : w + 1], (32, q)) & bits) != 0 for w in range(8)], axis=0
        )
        dscore = ((prob - jnp.where(target, 1.0, 0.0)) * (1.0 / QUERIES)).astype(jnp.bfloat16)
        dims = (((1,), (1,)), ((), ()))
        acc[lo] += lax.dot_general(dscore, near, dims, preferred_element_type=jnp.float32)
        acc[1 - lo] += lax.dot_general(dscore, far, dims, preferred_element_type=jnp.float32)
        return 0

    hop3("mid_up")
    hop3("mid_down")
    for name in ("own", "near_up", "near_down", "mid_up", "mid_down"):
        done(name)
    lax.fori_loop(2, 7, pair, 0)
    hop3("far_up")
    hop3("far_down")
    done("far_up")
    done("far_down")
    lax.fori_loop(7, 10, pair, 0)

    loads[3].wait()
    loads[4].wait()
    step_rows = 32

    def refresh(i, carry):
        at = pl.ds(pl.multiple_of(i * step_rows, step_rows), step_rows)
        totals = list(carry)
        for h in range(2):
            cols = slice(h * HALF, (h + 1) * HALF)
            g = acc[h, at] * SCALE
            w = w_in[at, cols]
            m = 0.9 * mom_in[at, cols] + 0.1 * g
            v = 0.999 * sec_in[at, cols] + 0.001 * g * g
            u = (m * (1.0 / (1.0 - 0.9**STEP))) / (
                jnp.sqrt(v * (1.0 / (1.0 - 0.999**STEP))) + 1e-06
            ) + 0.01 * w
            update_out[at, cols] = u
            moment_out[at, cols] = m
            second_out[at, cols] = v
            for k, s in enumerate((w * w, u * u)):
                s = jnp.sum(s.reshape(step_rows // 8, 8, HALF), axis=0)
                totals[k] += s[:, :128] + s[:, 128:256] + s[:, 256:]
        return tuple(totals)

    zero = jnp.zeros((8, 128), jnp.float32)
    totals = lax.fori_loop(0, ROWS // step_rows, refresh, (zero, zero))
    value = jnp.concatenate([jnp.sum(t, axis=0, keepdims=True) for t in totals], axis=0)

    base = 4
    for stage, (axis, n) in enumerate((("core", 2), ("x", NX), ("y", NY), ("z", NZ))):
        sums[stage] = value
        order = sorted(range(1, n), key=lambda d: -min(d, n - d))
        cs = [copy(sums.at[stage], sums.at[base + d - 1], along(axis, d)) for d in order]
        for c in cs:
            c.wait_recv()
        for d in range(1, n):
            value = value + sums[base + d - 1]
        base += n - 1
    norms = jnp.sqrt(jnp.sum(value, axis=1, keepdims=True))
    trust = norms[0:1] / (norms[1:2] + 1e-06)
    trust_out[...] = jnp.broadcast_to(trust, trust_out.shape)

    for c in sent:
        c.wait_send()


def shards(features, label_ids, label_count, weight, moment, second):
    anywhere = pl.BlockSpec(memory_space=pl.ANY)
    vmem = pl.BlockSpec(memory_space=pltpu.VMEM)
    f32, bf16, i32 = jnp.float32, jnp.bfloat16, jnp.int32
    block = jax.ShapeDtypeStruct(weight.shape, f32)
    update, new_moment, new_second, trust = pl.pallas_call(
        kernel,
        name="step",
        out_shape=(block, block, block, jax.ShapeDtypeStruct((8, 128), f32)),
        in_specs=[anywhere, anywhere, vmem, anywhere, anywhere, anywhere],
        out_specs=(vmem, vmem, vmem, vmem),
        scratch_shapes=[
            pltpu.VMEM(features.shape, bf16),
            pltpu.VMEM(label_ids.shape, i32),
            pltpu.VMEM((4, 8, BLOCK_Q), i32),
            pltpu.VMEM(weight.shape, f32),
            pltpu.VMEM(weight.shape, f32),
            pltpu.VMEM(weight.shape, f32),
            pltpu.VMEM((2, ROWS, HALF), bf16),
            pltpu.VMEM((NZ, NY, NX, 2, BLOCK_D, BLOCK_Q), bf16),
            pltpu.VMEM((8, NY, NX, 8, BLOCK_Q), i32),
            pltpu.VMEM((8, NY, 8, BLOCK_Q), i32),
            pltpu.VMEM((2, ROWS, HALF), f32),
            pltpu.VMEM((26, 2, 128), f32),
            pltpu.SemaphoreType.DMA((N_SEMS,)),
            pltpu.SemaphoreType.DMA((N_SEMS,)),
            pltpu.SemaphoreType.DMA((5,)),
        ],
        compiler_params=pltpu.CompilerParams(
            collective_id=0, has_side_effects=True, vmem_limit_bytes=40 << 20
        ),
    )(features, label_ids, label_count.reshape(1, -1), weight, moment, second)
    return (trust[0, 0] * update, new_moment, new_second)


def solution(mesh):
    in_specs = (
        P("dp", "label"),
        P("dp", None),
        P("dp"),
        P(("dp", "label"), None),
        P(("dp", "label"), None),
        P(("dp", "label"), None),
    )
    out_specs = (P(("dp", "label"), None), P(("dp", "label"), None), P(("dp", "label"), None))
    return jax.shard_map(shards, mesh=mesh, in_specs=in_specs, out_specs=out_specs, check_vma=False)
```

time: 441 us -> 85.3 us (0.19)
  blocking collectives: 383 us -> 0 us
  Pallas kernels: 0 us -> 75.6 us
  other arithmetic: 26.9 us -> 1.58 us
  between operations: 15.5 us -> 0.67 us
  matrix products: 14.3 us -> 0 us
  local copies, waits for them, and re-layouts: 0.6 us -> 7.15 us
    all_gather x3 -> x0, blocking collectives: 259 us -> none  [the longest x1 104 us: shards(): lax.all_gather(label_count, 'dp', axis=0, tiled=True)]
    psum x1 -> x0, blocking collectives: 125 us -> none  [shards(): lax.psum((jnp.sum(weight * weight), jnp.sum(update * update)), ('dp', 'la...]
    pallas_call x0 -> x1, Pallas kernels: none -> 75.6 us  [shards(): pl.pallas_call(kernel, name='step', out_shape=(block, block, block, jax.S...]
    reduce_or x1 -> x0, other arithmetic: 25.9 us -> none  [grad_piece(): jnp.any(local[:, :, None] == columns[None, None, :], axis=1)]
    dot_general x1 -> x0, matrix products: 14.3 us -> none  [grad_piece(): lax.dot_general(dscore, queries, (((0,), (0,)), ((), ())), preferred_elem...]
    unnamed x0 -> x14, local copies, waits for them, and re-layouts: none -> 6.63 us
  transfers between devices with their start and end apart: 1 -> 0, of which waited for: 0 -> 0; matrix products, arithmetic and copies ran while one was open for 6% -> 0% of each run, Pallas kernels for 0% -> 0%
where the time goes in v1:
time: 85.3 us; the launch traced here: 85 us
  Pallas kernels  75.6 us (89%)
  local copies, waits for them, and re-layouts  7.15 us (8%)
  other arithmetic  1.58 us (2%)
    pallas_call x1, Pallas kernels, shards(): pl.pallas_call(kernel, name='step', out_shape=(block, block, block, jax.S...  75.6 us
    unnamed x14, local copies, waits for them, and re-layouts  6.63 us

profile of v1, /device:TPU:1, one launch (start us, length us, event | category | flops | bytes accessed | tf_op | source)
XLA Modules:
  0.0 85.0 jit_solution(12663474712536952436)
XLA Ops:
  0.6 0.0 copy-start.4
  0.6 0.8 copy.9.features
  1.5 0.0 copy-done.4
  1.5 0.0 copy-start.3
  1.5 0.1 copy.10.ids
  1.6 0.6 copy-done.3
  2.1 0.0 copy-start
  2.1 1.1 %copy-done = f32[256,768]{1,0:T(8,128)S(1)} copy-done((f32[256,768]{1,0:T(8,128)S(1)}, f32[256,768]{1,0:T(8,128)}, u32[]{:S(2)}) %copy-start) | copy-done | bytes 786456
  3.3 0.0 copy-start.1
  3.3 1.1 %copy-done.1 = f32[256,768]{1,0:T(8,128)S(1)} copy-done((f32[256,768]{1,0:T(8,128)S(1)}, f32[256,768]{1,0:T(8,128)}, u32[]{:S(2)}) %copy-start.1) | copy-done | bytes 786456
  4.4 0.0 copy-start.2
  4.4 1.1 %copy-done.2 = f32[256,768]{1,0:T(8,128)S(1)} copy-done((f32[256,768]{1,0:T(8,128)S(1)}, f32[256,768]{1,0:T(8,128)}, u32[]{:S(2)}) %copy-start.2) | copy-done | bytes 786456
  5.5 75.6 %step.1 = (f32[256,768]{1,0:T(8,128)S(1)}, f32[256,768]{1,0:T(8,128)S(1)}, f32[256,768]{1,0:T(8,128)S(1)}, f32[8,128]{1,0:T(8,128)S(1)}) custom-call(bf16[128,48]{1,0:T(8,128)(2,1)S(1)} %copy.9.features, s32[128,32]{1,0:T(8,128)S(1)} %copy.10.ids, s32[1,128]{1,0:T(1,128)S(1)} %bitcast.2, f32[256,768]{1,0:T(8,128)S(1)} %copy-done, f32[256,768]{1,0:T(8,128)S(1)} %copy-done.1, ...), custom_call_target="tpu_custom_call" | custom-call | tf_op jit(solution)/shard_map/step/pallas_call | solution.py:300
  81.1 0.5 slice.3
  81.7 1.6 %broadcast_multiply_fusion = f32[256,768]{1,0:T(8,128)} fusion(f32[256,768]{1,0:T(8,128)S(1)} %get-tuple-element.8, f32[]{:T(128)} %bitcast.1), kind=kLoop, calls=%fused_computation | loop fusion | flops 196608 | bytes 1572868 | tf_op jit(solution)/shard_map/mul | solution.py:327
  83.2 0.9 %copy.13 = f32[256,768]{1,0:T(8,128)} copy(f32[256,768]{1,0:T(8,128)S(1)} %get-tuple-element.15) | data formatting | bytes 1572864
  84.1 0.9 %copy.14 = f32[256,768]{1,0:T(8,128)} copy(f32[256,768]{1,0:T(8,128)S(1)} %get-tuple-element.16) | data formatting | bytes 1572864
Async XLA Ops:
  0.6 0.8 copy-start.4
  1.5 0.7 copy-start.3
  2.1 1.1 %copy-start = (f32[256,768]{1,0:T(8,128)S(1)}, f32[256,768]{1,0:T(8,128)}, u32[]{:S(2)}) copy-start(f32[256,768]{1,0:T(8,128)} %weight.1) | copy-start | bytes 2359300
  3.3 1.1 %copy-start.1 = (f32[256,768]{1,0:T(8,128)S(1)}, f32[256,768]{1,0:T(8,128)}, u32[]{:S(2)}) copy-start(f32[256,768]{1,0:T(8,128)} %moment.1) | copy-start | bytes 2359300
  4.4 1.1 %copy-start.2 = (f32[256,768]{1,0:T(8,128)S(1)}, f32[256,768]{1,0:T(8,128)}, u32[]{:S(2)}) copy-start(f32[256,768]{1,0:T(8,128)} %second.1) | copy-start | bytes 2359300

commit v2 on v1

v2 whole, which is shorter than its diff:
```python
import jax
import jax.numpy as jnp
from jax import lax
from jax.experimental import pallas as pl
from jax.experimental.pallas import tpu as pltpu
from jax.sharding import PartitionSpec as P

STEP = 10
MESH = pl.DeviceIdType.MESH
NX, NY, NZ = 4, 4, 16
WIDTH, ROWS, QUERIES = 768, 256, 4096
HALF = WIDTH // 2
BLOCK_D, BLOCK_Q = 48, 128
SCALE = 1.0 / WIDTH**0.5
LOG2_E = 1.4426950408889634
N_SEMS = 220

GROUPS = {
    "own": (0, 1, "y"),
    "4": (4, 5, "x"),
    "12": (12, 13, "y"),
    "5": (5, 6, "x"),
    "11": (11, 12, "y"),
    "6": (6, 7, "x"),
    "10": (10, 11, "y"),
    "78": (7, 9, "x"),
    "9": (9, 10, "y"),
}
LAST = ("5", "11")
Z_ORDER = (8, 7, 9, 4, 12, 6, 10, 5, 11)
OTHERS = (1, 3, 2)
Z_FAR_FIRST = (8, 7, 9, 6, 10, 5, 11, 4, 12, 3, 13, 2, 14, 1, 15)
PLANE = sorted(
    ((i, j, k) for i in range(NX) for j in range(NY) for k in range(2) if i or j or k),
    key=lambda o: -(min(o[0], NX - o[0]) + min(o[1], NY - o[1]) + o[2]),
)


def kernel(
    features, ids, count, weight, moment, second,
    update_out, moment_out, second_out, trust_out,
    feat_in, ids_in, ids_t, w_in, mom_in, sec_in, w_bf, held, labels, words, acc, sums,
    send, recv, local,
):
    dp, lb = lax.axis_index("dp"), lax.axis_index("label")
    x, y, core = lax.rem(lb // 2, NX), lax.rem(dp, NY), lax.rem(lb, 2)
    z = (lb // 8) * 8 + dp // NY

    def device(x, y, z, core):
        return {"dp": lax.rem(z, 8) * NY + y, "label": (z // 8) * 8 + x * 2 + core}

    def along(axis, by):
        if axis == "x":
            return device(lax.rem(x + by, NX), y, z, core)
        if axis == "y":
            return device(x, lax.rem(y + by, NY), z, core)
        if axis == "z":
            return device(x, y, lax.rem(z + by, NZ), core)
        return device(x, y, z, 1 - core)

    def in_plane(offset):
        i, j, k = offset
        return device(lax.rem(x + i, NX), lax.rem(y + j, NY), z, lax.rem(core + k, 2))

    barrier = pltpu.get_barrier_semaphore()
    for by in Z_FAR_FIRST:
        pl.semaphore_signal(barrier, inc=1, device_id=along("z", by), device_id_type=MESH)
    for offset in PLANE:
        pl.semaphore_signal(barrier, inc=1, device_id=in_plane(offset), device_id_type=MESH)

    loads = []
    for i, (src, dst) in enumerate(
        [(features, feat_in), (ids, ids_in), (weight, w_in), (moment, mom_in), (second, sec_in)]
    ):
        loads.append(pltpu.make_async_copy(src, dst, local.at[i]))
        loads[-1].start()

    loads[0].wait()
    held[0, y, x, core] = feat_in[...]
    loads[1].wait()
    used = lax.broadcasted_iota(jnp.int32, ids_in.shape, 0) < count[...]
    ids_t[...] = jnp.where(used, ids_in[...], -1).reshape(4, 8, BLOCK_Q)
    row, col = jnp.where(core == 0, y, x), jnp.where(core == 0, x, y)
    labels[3 + 5 * core, row, col] = ids_t[x]
    loads[2].wait()
    w_bf[0] = w_in[:, :HALF].astype(jnp.bfloat16)
    w_bf[1] = w_in[:, HALF:].astype(jnp.bfloat16)
    acc[...] = jnp.zeros_like(acc)

    used_sems, sent = [0], []

    def sems():
        used_sems[0] += 1
        return send.at[used_sems[0] - 1], recv.at[used_sems[0] - 1]

    def copy(src, dst, to, recv_sem=None):
        s, r = sems()
        c = pltpu.make_async_remote_copy(
            src, dst, s, r if recv_sem is None else recv_sem, device_id=to, device_id_type=MESH
        )
        sent.append(c)
        c.start()
        return c

    def arrived(part, sem):
        pltpu.make_async_remote_copy(
            part, part, send.at[0], sem, device_id=along("z", 1), device_id_type=MESH
        ).wait_recv()

    pl.semaphore_wait(barrier, len(Z_FAR_FIRST) + len(PLANE))

    toward = 1 - 2 * core
    label_z = sems()[1]
    for k in (3, 2, 1, 0):
        to = device(x, y, lax.rem(z + toward * (k + 1) + NZ, NZ), core)
        there = 8 - core if k == 3 else (2 - k) * (1 - core) + (4 + k) * core
        copy(ids_t.at[x], labels.at[there, row, col], to, label_z)

    def label_hop(first, i):
        on_x = (core == 0) == first
        return device(
            jnp.where(on_x, lax.rem(x + i, NX), x), jnp.where(on_x, y, lax.rem(y + i, NY)), z, core
        )

    z_recv = {name: sems()[1] for name in GROUPS if name != "own"}
    for d in Z_ORDER:
        there = NZ - d
        name = next(n for n, (a, b, _) in GROUPS.items() if a <= there < b)
        copy(held.at[0, y, x, core], held.at[there, y, x, core], along("z", d), z_recv[name])

    hops, cross = {}, {}

    def hop1(name):
        a, b, axis = GROUPS[name]
        part = held.at[a:b, y, x, core]
        if name != "own":
            arrived(part, z_recv[name])
        hops[name] = [copy(part, part, along(axis, i)) for i in OTHERS]

    def line(name, at):
        a, b, axis = GROUPS[name]
        return held.at[a:b, at, :, core] if axis == "x" else held.at[a:b, :, at, core]

    def to_core(name, part):
        cross.setdefault(name, []).append(copy(part, part, along("core", 1)))

    passed = [[], [], []]

    def to_z(k, at):
        ups = held.at[(NZ - k) % NZ, :, at, core], held.at[NZ - 1 - k, :, at, core]
        downs = held.at[k, :, at, core], held.at[k + 1, :, at, core]
        passed[k].append((copy(*ups, along("z", 1)), copy(*downs, along("z", NZ - 1))))

    def from_z(k, n):
        at = lax.rem(x + 4 - (0, *OTHERS)[n], 4)
        for c in passed[k][n]:
            c.wait_recv()
        if k < 2:
            to_z(k + 1, at)
        for r in (k + 1, NZ - 1 - k):
            if k == 2:
                to_core("z3", held.at[r, :, at, core])
            elif n == 3:
                to_core("z" + str(k + 1), held.at[r, :, :, core])

    def hop2(name):
        other, mine = ("y", y) if GROUPS[name][2] == "x" else ("x", x)
        for c in hops[name]:
            c.wait_recv()
        part = line(name, mine)
        hops[name] = [copy(part, part, along(other, i)) for i in OTHERS]
        if name == "own":
            to_z(0, mine)
        if name in LAST:
            to_core(name, part)

    def hop3(name):
        a, b, axis = GROUPS[name]
        mine = y if axis == "x" else x
        for c, i in zip(hops[name], OTHERS, strict=True):
            c.wait_recv()
            at = lax.rem(mine + 4 - i, 4)
            if name == "own":
                to_z(0, at)
            if name in LAST:
                to_core(name, line(name, at))
        if name not in LAST:
            for r in range(a, b):
                to_core(name, held.at[r, :, :, core])

    def done(name):
        for c in cross[name]:
            c.wait_recv()

    def label_send(part, to):
        return [copy(part, part, d) for d in to]

    hop1("own")
    hop2("own")
    arrived(labels.at[0:4, row, col], label_z)
    part = labels.at[pl.ds(4 * core, 4), row, col]
    label_sent = label_send(part, [label_hop(True, i) for i in OTHERS])
    hop1("4")
    hop1("12")
    hop3("own")
    hop1("5")
    hop1("11")
    hop1("6")
    hop1("10")
    hop1("78")
    hop1("9")
    hop2("4")
    hop2("12")
    for c in label_sent:
        c.wait_recv()
    part = labels.at[pl.ds(4 * core, 4), row]
    label_sent = label_send(part, [label_hop(False, i) for i in OTHERS])
    from_z(0, 0)
    from_z(0, 1)
    hop2("6")
    hop2("10")
    from_z(0, 2)
    from_z(0, 3)
    hop2("78")
    hop2("9")
    hop2("5")
    hop2("11")
    for c in label_sent:
        c.wait_recv()
    label_sent = []
    for i in range(2):
        label_sent += label_send(labels.at[pl.ds(4 * core + 2 * i, 2)], [along("core", 1)])
    from_z(1, 0)
    from_z(1, 1)
    hop3("4")
    hop3("12")

    for c in label_sent:
        c.wait_recv()
    first = (dp * 16 + lb) * ROWS

    def mark(i, core):
        pos, at = i // NY, lax.rem(i, NY)
        if core == 0:
            pair, found = lax.rem(pos + 5, 8), labels[pos, at]
        else:
            pair, found = pos + 1, labels[4 + pos, :, at]
        local_id = found - first
        word = local_id >> 5
        bit = jnp.left_shift(jnp.int32(1), local_id & 31)
        rows = lax.broadcasted_iota(jnp.int32, (8, BLOCK_Q), 0)
        out = jnp.zeros((8, BLOCK_Q), jnp.int32)
        for w in range(8):
            hit = jnp.where(word == w, bit, 0)
            hit = (hit[0] | hit[1]) | (hit[2] | hit[3])
            for by in (4, 2, 1):
                hit = hit | pltpu.roll(hit, by, 0)
            out = jnp.where(rows == w, hit, out)
        words[pair, at] = out
        return core

    for i in range(2):
        lax.fori_loop(0, 4 * NY, lambda n, _, i=i: (mark(n, i), 0)[1], 0)

    def pair(r):
        lo = lax.rem(z + r, NZ) // 8
        q = NY * BLOCK_Q

        def slab(at):
            return jnp.concatenate([held[at, i].reshape(HALF, BLOCK_Q) for i in range(NY)], axis=1)

        near, far = slab(r), slab(r + 8)
        scores = jnp.dot(
            jnp.concatenate([w_bf[lo], w_bf[1 - lo]], axis=1),
            jnp.concatenate([near, far], axis=0),
            preferred_element_type=jnp.float32,
        )
        prob = 1.0 / (1.0 + jnp.exp2(scores * (-SCALE * LOG2_E)))
        marks = jnp.concatenate([words[r, i] for i in range(NY)], axis=1)
        bits = jnp.left_shift(jnp.int32(1), lax.broadcasted_iota(jnp.int32, (32, q), 0))
        target = jnp.concatenate(
            [(jnp.broadcast_to(marks[w : w + 1], (32, q)) & bits) != 0 for w in range(8)], axis=0
        )
        dscore = (prob - jnp.where(target, 1.0, 0.0)).astype(jnp.bfloat16)
        dims = (((1,), (1,)), ((), ()))
        acc[lo] += lax.dot_general(dscore, near, dims, preferred_element_type=jnp.float32)
        acc[1 - lo] += lax.dot_general(dscore, far, dims, preferred_element_type=jnp.float32)

    def pairs(first_r, by, n):
        def one(i, _):
            pair(lax.rem(first_r + i * by, 8))
            return 0

        lax.fori_loop(0, n, one, 0)

    from_z(1, 2)
    from_z(1, 3)
    done("4")
    done("12")
    pairs(4, 1, 1)
    hop3("6")
    hop3("10")
    done("6")
    done("10")
    done("z2")
    from_z(2, 0)
    pairs(2, 4, 2)
    hop3("78")
    hop3("9")
    from_z(2, 1)
    for name in ("own", "z1", "78", "9"):
        done(name)
    pairs(7, 1, 3)
    hop3("5")
    hop3("11")
    from_z(2, 2)
    from_z(2, 3)
    for name in ("z3", "5", "11"):
        done(name)
    pairs(3, 2, 2)

    loads[3].wait()
    loads[4].wait()
    step_rows = 32

    def refresh(i, carry):
        at = pl.ds(pl.multiple_of(i * step_rows, step_rows), step_rows)
        totals = list(carry)
        for h in range(2):
            cols = slice(h * HALF, (h + 1) * HALF)
            g = acc[h, at] * (SCALE / QUERIES)
            w = w_in[at, cols]
            m = 0.9 * mom_in[at, cols] + 0.1 * g
            v = 0.999 * sec_in[at, cols] + 0.001 * g * g
            u = (m * (1.0 / (1.0 - 0.9**STEP))) / (
                jnp.sqrt(v * (1.0 / (1.0 - 0.999**STEP))) + 1e-06
            ) + 0.01 * w
            update_out[at, cols] = u
            moment_out[at, cols] = m
            second_out[at, cols] = v
            for k, s in enumerate((w * w, u * u)):
                s = jnp.sum(s.reshape(step_rows // 8, 8, HALF), axis=0)
                totals[k] += s[:, :128] + s[:, 128:256] + s[:, 256:]
        return tuple(totals)

    zero = jnp.zeros((8, 128), jnp.float32)
    totals = lax.fori_loop(0, ROWS // step_rows, refresh, (zero, zero))
    value = jnp.concatenate([jnp.sum(t, axis=0, keepdims=True) for t in totals], axis=0)

    base = 2
    to_plane = [in_plane(o) for o in PLANE]
    to_column = [along("z", by) for by in Z_FAR_FIRST]
    for stage, to in enumerate((to_plane, to_column)):
        sums[stage] = value
        cs = [copy(sums.at[stage], sums.at[base + i], d) for i, d in enumerate(to)]
        for c in cs:
            c.wait_recv()
        value = value + jnp.sum(sums[base : base + len(to)], axis=0)
        base += len(to)
    norms = jnp.sqrt(jnp.sum(value, axis=1, keepdims=True))
    trust = norms[0:1] / (norms[1:2] + 1e-06)
    trust_out[...] = jnp.broadcast_to(trust, trust_out.shape)

    for c in sent:
        c.wait_send()


def finish(update, moment, second, trust, step_out, moment_out, second_out, scaled, done):
    copies = [
        pltpu.make_async_copy(moment, moment_out, done.at[0]),
        pltpu.make_async_copy(second, second_out, done.at[1]),
    ]
    for c in copies:
        c.start()
    n = ROWS // 4
    for i in range(4):
        at = pl.ds(i * n, n)
        scaled[at] = update[at] * trust[0:1, 0:1]
        copies.append(pltpu.make_async_copy(scaled.at[at], step_out.at[at], done.at[2 + i]))
        copies[-1].start()
    for c in copies:
        c.wait()


def shards(features, label_ids, label_count, weight, moment, second):
    hbm = pl.BlockSpec(memory_space=pltpu.HBM)
    vmem = pl.BlockSpec(memory_space=pltpu.VMEM)
    f32, bf16, i32 = jnp.float32, jnp.bfloat16, jnp.int32
    block = jax.ShapeDtypeStruct(weight.shape, f32)
    results = pl.pallas_call(
        kernel,
        name="step",
        out_shape=(block, block, block, jax.ShapeDtypeStruct((8, 128), f32)),
        in_specs=[hbm, hbm, vmem, hbm, hbm, hbm],
        out_specs=(vmem, vmem, vmem, vmem),
        scratch_shapes=[
            pltpu.VMEM(features.shape[::-1], bf16),
            pltpu.VMEM(label_ids.shape[::-1], i32),
            pltpu.VMEM((4, 8, BLOCK_Q), i32),
            pltpu.VMEM(weight.shape, f32),
            pltpu.VMEM(weight.shape, f32),
            pltpu.VMEM(weight.shape, f32),
            pltpu.VMEM((2, ROWS, HALF), bf16),
            pltpu.VMEM((NZ, NY, NX, 2, BLOCK_D, BLOCK_Q), bf16),
            pltpu.VMEM((9, NY, NX, 8, BLOCK_Q), i32),
            pltpu.VMEM((8, NY, 8, BLOCK_Q), i32),
            pltpu.VMEM((2, ROWS, HALF), f32),
            pltpu.VMEM((48, 2, 128), f32),
            pltpu.SemaphoreType.DMA((N_SEMS,)),
            pltpu.SemaphoreType.DMA((N_SEMS,)),
            pltpu.SemaphoreType.DMA((5,)),
        ],
        compiler_params=pltpu.CompilerParams(
            collective_id=0, has_side_effects=True, vmem_limit_bytes=411 << 17
        ),
    )(features.T, label_ids.T, label_count.reshape(1, -1), weight, moment, second)
    return pl.pallas_call(
        finish,
        name="finish",
        out_shape=(block, block, block),
        in_specs=[vmem] * 4,
        out_specs=(hbm, hbm, hbm),
        scratch_shapes=[pltpu.VMEM(weight.shape, f32), pltpu.SemaphoreType.DMA((6,))],
        compiler_params=pltpu.CompilerParams(vmem_limit_bytes=8 << 20),
    )(*results)


def solution(mesh):
    in_specs = (
        P("dp", "label"),
        P("dp", None),
        P("dp"),
        P(("dp", "label"), None),
        P(("dp", "label"), None),
        P(("dp", "label"), None),
    )
    out_specs = (P(("dp", "label"), None), P(("dp", "label"), None), P(("dp", "label"), None))
    return jax.shard_map(shards, mesh=mesh, in_specs=in_specs, out_specs=out_specs, check_vma=False)
```

time: 85.3 us -> 72.1 us (0.85)
  Pallas kernels: 75.6 us -> 69.1 us
  local copies, waits for them, and re-layouts: 7.15 us -> 2.07 us
  other arithmetic: 1.58 us -> 0 us
    pallas_call x1, Pallas kernels: 75.6 us -> 67.7 us  [shards(): pl.pallas_call(kernel, name='step', out_shape=(block, block, block, jax.S...]
    unnamed x14 -> x6, local copies, waits for them, and re-layouts: 6.63 us -> 2.07 us
    mul x1 -> x0, other arithmetic: 1.58 us -> none  [shards(): return (trust[0, 0] * update, new_moment, new_second)]
    pallas_call x0 -> x1, Pallas kernels: none -> 1.44 us  [shards(): pl.pallas_call(finish, name='finish', out_shape=(block, block, block), in...]
where the time goes in v2:
time: 72.1 us; the launch traced here: 71.9 us
  Pallas kernels  69.1 us (96%)
  local copies, waits for them, and re-layouts  2.07 us (3%)
    pallas_call x1, Pallas kernels, shards(): pl.pallas_call(kernel, name='step', out_shape=(block, block, block, jax.S...  67.7 us
    unnamed x6, local copies, waits for them, and re-layouts  2.07 us
    pallas_call x1, Pallas kernels, shards(): pl.pallas_call(finish, name='finish', out_shape=(block, block, block), in...  1.44 us

profile of v2, /device:TPU:1, one launch (start us, length us, event | category | flops | bytes accessed | tf_op | source)
XLA Modules:
  0.0 71.9 jit_solution(15211317674128039537)
XLA Ops:
  0.6 0.0 copy-start.2
  0.6 0.6 copy-done.2
  1.3 0.0 copy-start
  1.3 0.7 copy-done
  2.0 0.0 copy-start.1
  2.0 0.7 copy-done.1
  2.7 67.7 %step.1 = (f32[256,768]{1,0:T(8,128)S(1)}, f32[256,768]{1,0:T(8,128)S(1)}, f32[256,768]{1,0:T(8,128)S(1)}, f32[8,128]{1,0:T(8,128)S(1)}) custom-call(bf16[48,128]{1,0:T(8,128)(2,1)S(1)} %bitcast.4, s32[32,128]{1,0:T(8,128)S(1)} %bitcast.3, s32[1,128]{1,0:T(1,128)S(1)} %bitcast.5, f32[256,768]{1,0:T(8,128)} %weight.1, f32[256,768]{1,0:T(8,128)} %moment.1, ...), custom_call_target="tpu_custom_call" | custom-call | tf_op jit(solution)/shard_map/step/pallas_call | solution.py:390
  70.4 1.4 %finish.1 = (f32[256,768]{1,0:T(8,128)}, f32[256,768]{1,0:T(8,128)}, f32[256,768]{1,0:T(8,128)}) custom-call(f32[256,768]{1,0:T(8,128)S(1)} %get-tuple-element.7.update, f32[256,768]{1,0:T(8,128)S(1)} %get-tuple-element.8.moment, f32[256,768]{1,0:T(8,128)S(1)} %get-tuple-element.9.second, f32[8,128]{1,0:T(8,128)S(1)} %get-tuple-element.10.trust), custom_call_target="tpu_custom_call" | custom-call | tf_op jit(solution)/shard_map/finish/pallas_call | solution.py:417
Async XLA Ops:
  0.6 0.7 copy-start.2
  1.3 0.7 copy-start
  2.0 0.7 copy-start.1

commit v3 on v2

v3 whole, which is shorter than its diff:
```python
import jax
import jax.numpy as jnp
from jax import lax
from jax.experimental import pallas as pl
from jax.experimental.pallas import tpu as pltpu
from jax.sharding import PartitionSpec as P

STEP = 10
MESH = pl.DeviceIdType.MESH
NX, NY, NZ = 4, 4, 16
WIDTH, ROWS, QUERIES = 768, 256, 4096
HALF = WIDTH // 2
BLOCK_D, BLOCK_Q = 48, 128
SCALE = 1.0 / WIDTH**0.5
LOG2_E = 1.4426950408889634
N_SEMS = 230

GROUPS = {
    "own": (0, 1, "y"),
    "4": (4, 5, "x"),
    "12": (12, 13, "y"),
    "5": (5, 6, "x"),
    "11": (11, 12, "y"),
    "6": (6, 7, "x"),
    "10": (10, 11, "y"),
    "78": (7, 9, "x"),
    "9": (9, 10, "y"),
}
FORWARDED = ()
LAST = ("5", "11")
Z_ORDER = (5, 12, 9, 4, 7, 6, 11, 10, 8)
OTHERS = (1, 3, 2)
Z_FAR_FIRST = (8, 7, 9, 6, 10, 5, 11, 4, 12, 3, 13, 2, 14, 1, 15)
ROW = ((2, 1), (2, 0), (1, 1), (3, 1), (1, 0), (3, 0), (0, 1))

ORDER = (
    ("h1", "own"), ("h2", "own"), ("lab", 0), ("h1", "4"), ("lab", 1), ("h1", "12"), ("h3", "own"),
    ("h1", "11"), ("h1", "5"), ("h1", "10"), ("h1", "6"), ("h2", "4"), ("h1", "78"), ("h1", "9"),
    ("fz", 0, 0), ("h2", "12"), ("lab", 2), ("h2", "11"), ("h2", "5"), ("h2", "10"), ("h2", "6"),
    ("fz", 0, 1), ("fz", 0, 2), ("lab", 3), ("fz", 0, 3), ("fz", 1, 0), ("h2", "9"), ("h2", "78"),
    ("h3", "4"), ("fz", 1, 1), ("fz", 1, 2), ("h3", "12"), ("fz", 1, 3), ("fz", 2, 0), ("h3", "5"),
    ("h3", "6"), ("p", 4), ("fz", 2, 1), ("h3", "10"), ("h3", "11"), ("h3", "9"), ("p", 6),
    ("fz", 2, 2), ("fz", 2, 3), ("p", 2), ("h3", "78"), ("p", 1, 5, 3), ("p", 0, 7),
)


def kernel(
    features, ids, count, weight, moment, second,
    update_hbm, moment_hbm, second_hbm, trust_hbm,
    feat_in, ids_in, count_in, ids_t, w_in, mom_in, sec_in, w_bf, held, labels, words, acc, sums,
    update_out, moment_out, second_out, trust_out, send, recv, local,
):
    dp, lb = lax.axis_index("dp"), lax.axis_index("label")
    x, y, core = lax.rem(lb // 2, NX), lax.rem(dp, NY), lax.rem(lb, 2)
    z = (lb // 8) * 8 + dp // NY

    def device(x, y, z, core):
        return {"dp": lax.rem(z, 8) * NY + y, "label": (z // 8) * 8 + x * 2 + core}

    def along(axis, by):
        if axis == "x":
            return device(lax.rem(x + by, NX), y, z, core)
        if axis == "y":
            return device(x, lax.rem(y + by, NY), z, core)
        if axis == "z":
            return device(x, y, lax.rem(z + by, NZ), core)
        return device(x, y, z, 1 - core)

    def in_row(by, cores):
        return device(lax.rem(x + by, NX), y, z, lax.rem(core + cores, 2))

    loads = {}
    for i, (name, src, dst) in enumerate(
        [
            ("features", features, feat_in),
            ("ids", ids, ids_in),
            ("count", count, count_in),
            ("weight", weight, w_in),
            ("moment", moment, mom_in),
            ("second", second, sec_in),
        ]
    ):
        loads[name] = pltpu.make_async_copy(src, dst, local.at[i])
        loads[name].start()

    barrier = pltpu.get_barrier_semaphore()
    column = [along("z", by) for by in Z_FAR_FIRST]
    file = [along("y", by) for by in (2, 1, 3)]
    row_ = [in_row(*o) for o in ROW]
    greeted = column + file + row_
    for to in greeted:
        pl.semaphore_signal(barrier, inc=1, device_id=to, device_id_type=MESH)

    loads["features"].wait()
    held[0, y, x, core] = feat_in[...]
    loads["ids"].wait()
    loads["count"].wait()
    used = lax.broadcasted_iota(jnp.int32, ids_in.shape, 0) < count_in[...]
    ids_t[...] = jnp.where(used, ids_in[...], -1).reshape(4, 8, BLOCK_Q)
    row, col = jnp.where(core == 0, y, x), jnp.where(core == 0, x, y)
    labels[3 + 5 * core, row, col] = ids_t[x]

    used_sems, sent = [0], []

    def sems():
        used_sems[0] += 1
        return send.at[used_sems[0] - 1], recv.at[used_sems[0] - 1]

    def copy(src, dst, to, recv_sem=None):
        s, r = sems()
        c = pltpu.make_async_remote_copy(
            src, dst, s, r if recv_sem is None else recv_sem, device_id=to, device_id_type=MESH
        )
        sent.append(c)
        c.start()
        return c

    def arrived(part, sem):
        pltpu.make_async_remote_copy(
            part, part, send.at[0], sem, device_id=along("z", 1), device_id_type=MESH
        ).wait_recv()

    pl.semaphore_wait(barrier, len(greeted))

    toward = 1 - 2 * core
    label_z = sems()[1]
    for k in (3, 2, 1, 0):
        to = device(x, y, lax.rem(z + toward * (k + 1) + NZ, NZ), core)
        there = 8 - core if k == 3 else (2 - k) * (1 - core) + (4 + k) * core
        copy(ids_t.at[x], labels.at[there, row, col], to, label_z)

    def label_hop(first, i):
        on_x = (core == 0) == first
        return device(
            jnp.where(on_x, lax.rem(x + i, NX), x), jnp.where(on_x, y, lax.rem(y + i, NY)), z, core
        )

    z_recv = {name: sems()[1] for name in GROUPS if name != "own"}
    for d in Z_ORDER:
        there = NZ - d
        name = next(n for n, (a, b, _) in GROUPS.items() if a <= there < b)
        copy(held.at[0, y, x, core], held.at[there, y, x, core], along("z", d), z_recv[name])

    hops, cross = {}, {}

    def hop1(name):
        a, b, axis = GROUPS[name]
        part = held.at[a:b, y, x, core]
        if name != "own":
            arrived(part, z_recv[name])
        hops[name] = [copy(part, part, along(axis, i)) for i in OTHERS]

    def line(name, at, part=slice(0, 4)):
        a, b, axis = GROUPS[name]
        return held.at[a:b, at, part, core] if axis == "x" else held.at[a:b, part, at, core]

    def to_core(name, part):
        cross.setdefault(name, []).append(copy(part, part, along("core", 1)))

    passed = [[], [], []]

    def to_z(k, at):
        ups = held.at[(NZ - k) % NZ, :, at, core], held.at[NZ - 1 - k, :, at, core]
        downs = held.at[k, :, at, core], held.at[k + 1, :, at, core]
        passed[k].append((copy(*ups, along("z", 1)), copy(*downs, along("z", NZ - 1))))

    def from_z(k, n):
        at = lax.rem(x + 4 - (0, *OTHERS)[n], 4)
        for c in passed[k][n]:
            c.wait_recv()
        if k < 2:
            to_z(k + 1, at)
        for r in (k + 1, NZ - 1 - k):
            if k == 2:
                to_core("z3", held.at[r, :, at, core])
            elif n == 3:
                to_core("z" + str(k + 1), held.at[r, :, :, core])

    def hop2(name):
        other, mine = ("y", y) if GROUPS[name][2] == "x" else ("x", x)
        for c in hops[name]:
            c.wait_recv()
        part = line(name, mine)
        to = OTHERS[:2] if name in FORWARDED else OTHERS
        hops[name] = [copy(part, part, along(other, i)) for i in to]
        if name == "own":
            to_z(0, mine)
        if name in LAST:
            to_core(name, part)

    def forward(name):
        other, mine = ("y", y) if GROUPS[name][2] == "x" else ("x", x)
        halves = []
        for c, i in zip(hops[name], OTHERS[:2], strict=True):
            c.wait_recv()
            at = lax.rem(mine + 4 - i, 4)
            part = line(name, at, slice(0, 2) if i == 1 else slice(2, 4))
            halves.append(copy(part, part, along(other, i)))
            if name in LAST:
                to_core(name, line(name, at))
        hops[name] = halves

    def hop3(name):
        a, b, axis = GROUPS[name]
        mine = y if axis == "x" else x
        for c, i in zip(hops[name], OTHERS, strict=False):
            c.wait_recv()
            at = lax.rem(mine + 4 - i, 4)
            if name == "own":
                to_z(0, at)
            if name in LAST and name not in FORWARDED:
                to_core(name, line(name, at))
        if name not in LAST:
            for r in range(a, b):
                to_core(name, held.at[r, :, :, core])
        elif name in FORWARDED:
            to_core(name, line(name, lax.rem(mine + 2, 4)))

    waiting = set()

    def done(name):
        if name not in waiting:
            waiting.add(name)
            for c in cross[name]:
                c.wait_recv()

    def slot(r):
        found = [n for n, (a, b, _) in GROUPS.items() if a <= r < b]
        return found[0] if found else "z" + str(min(r, NZ - r))

    first = (dp * 16 + lb) * ROWS

    def mark(i, core):
        pos, at = i // NY, lax.rem(i, NY)
        if core == 0:
            pair, found = lax.rem(pos + 5, 8), labels[pos, at]
        else:
            pair, found = pos + 1, labels[4 + pos, :, at]
        local_id = found - first
        word = local_id >> 5
        bit = jnp.left_shift(jnp.int32(1), local_id & 31)
        rows = lax.broadcasted_iota(jnp.int32, (8, BLOCK_Q), 0)
        out = jnp.zeros((8, BLOCK_Q), jnp.int32)
        for w in range(8):
            hit = jnp.where(word == w, bit, 0)
            hit = (hit[0] | hit[1]) | (hit[2] | hit[3])
            for by in (4, 2, 1):
                hit = hit | pltpu.roll(hit, by, 0)
            out = jnp.where(rows == w, hit, out)
        words[pair, at] = out
        return core

    label_sent = []

    def label(stage):
        if stage == 0:
            arrived(labels.at[0:4, row, col], label_z)
        for c in label_sent:
            c.wait_recv()
        label_sent.clear()
        if stage == 0:
            part = labels.at[pl.ds(4 * core, 4), row, col]
            label_sent.extend(copy(part, part, label_hop(True, i)) for i in OTHERS)
        elif stage == 1:
            part = labels.at[pl.ds(4 * core, 4), row]
            label_sent.extend(copy(part, part, label_hop(False, i)) for i in OTHERS)
        elif stage == 2:
            part = labels.at[pl.ds(4 * core, 4)]
            label_sent.append(copy(part, part, along("core", 1)))
        else:
            for i in range(2):
                lax.fori_loop(0, 4 * NY, lambda n, _, i=i: (mark(n, i), 0)[1], 0)

    def pair(r):
        lo = lax.rem(z + r, NZ) // 8
        q = NY * BLOCK_Q

        def slab(at):
            return jnp.concatenate([held[at, i].reshape(HALF, BLOCK_Q) for i in range(NY)], axis=1)

        block = jnp.concatenate([slab(r), slab(r + 8)], axis=0)
        both = jnp.concatenate([w_bf[lo], w_bf[1 - lo]], axis=1)
        scores = jnp.dot(both, block, preferred_element_type=jnp.float32)
        prob = 1.0 / (1.0 + jnp.exp2(scores * (-SCALE * LOG2_E)))
        marks = jnp.concatenate([words[r, i] for i in range(NY)], axis=1)
        bits = jnp.left_shift(jnp.int32(1), lax.broadcasted_iota(jnp.int32, (32, q), 0))
        target = jnp.concatenate(
            [(jnp.broadcast_to(marks[w : w + 1], (32, q)) & bits) != 0 for w in range(8)], axis=0
        )
        dscore = (prob - jnp.where(target, 1.0, 0.0)).astype(jnp.bfloat16)
        dims = (((1,), (1,)), ((), ()))
        g = lax.dot_general(dscore, block, dims, preferred_element_type=jnp.float32)
        acc[lo] += g[:, :HALF]
        acc[1 - lo] += g[:, HALF:]

    steps = {"h1": hop1, "h2": hop2, "h2b": forward, "h3": hop3, "fz": from_z, "lab": label}
    for at, (what, *args) in enumerate(ORDER):
        if at == 2:
            loads["weight"].wait()
            w_bf[0] = w_in[:, :HALF].astype(jnp.bfloat16)
            w_bf[1] = w_in[:, HALF:].astype(jnp.bfloat16)
            acc[...] = jnp.zeros_like(acc)
        if what != "p":
            steps[what](*args)
            continue
        for r in args:
            done(slot(r))
            done(slot(r + 8))
        for r in args:
            pair(r)

    loads["moment"].wait()
    loads["second"].wait()
    step_rows = 32

    def refresh(i, carry):
        at = pl.ds(pl.multiple_of(i * step_rows, step_rows), step_rows)
        totals = list(carry)
        for h in range(2):
            cols = slice(h * HALF, (h + 1) * HALF)
            g = acc[h, at] * (SCALE / QUERIES)
            w = w_in[at, cols]
            m = 0.9 * mom_in[at, cols] + 0.1 * g
            v = 0.999 * sec_in[at, cols] + 0.001 * g * g
            u = (m * (1.0 / (1.0 - 0.9**STEP))) / (
                jnp.sqrt(v * (1.0 / (1.0 - 0.999**STEP))) + 1e-06
            ) + 0.01 * w
            update_out[at, cols] = u
            moment_out[at, cols] = m
            second_out[at, cols] = v
            for k, s in enumerate((w * w, u * u)):
                s = jnp.sum(s.reshape(step_rows // 8, 8, HALF), axis=0)
                totals[k] += s[:, :128] + s[:, 128:256] + s[:, 256:]
        return tuple(totals)

    zero = jnp.zeros((8, 128), jnp.float32)
    totals = lax.fori_loop(0, ROWS // step_rows, refresh, (zero, zero))
    stores = [
        pltpu.make_async_copy(update_out, update_hbm, local.at[6]),
        pltpu.make_async_copy(moment_out, moment_hbm, local.at[7]),
        pltpu.make_async_copy(second_out, second_hbm, local.at[8]),
    ]
    for c in stores:
        c.start()
    value = jnp.concatenate([jnp.sum(t, axis=0, keepdims=True) for t in totals], axis=0)

    base = 3
    for stage, to in enumerate((row_, file, column)):
        sums[stage] = value
        cs = [copy(sums.at[stage], sums.at[base + i], d) for i, d in enumerate(to)]
        for c in cs:
            c.wait_recv()
        value = value + jnp.sum(sums[base : base + len(to)], axis=0)
        base += len(to)
    norms = jnp.sqrt(jnp.sum(value, axis=1, keepdims=True))
    trust = norms[0:1] / (norms[1:2] + 1e-06)
    trust_out[...] = jnp.broadcast_to(trust, trust_out.shape)
    store = pltpu.make_async_copy(trust_out, trust_hbm, local.at[0])
    store.start()
    for c in sent:
        c.wait_send()
    for c in stores:
        c.wait()
    store.wait()


def finish(update, moment, second, trust, step_out, moment_out, second_out, held, scaled, by, given, done):
    parts, n = 4, ROWS // 4
    factor = pltpu.make_async_copy(trust, by, given.at[3, 0])
    factor.start()
    reads, writes = {}, []
    for i in range(parts):
        at = pl.ds(i * n, n)
        for k, src in enumerate((update, moment, second)):
            reads[k, i] = pltpu.make_async_copy(src.at[at], held.at[k, at], given.at[k, i])
            reads[k, i].start()
    factor.wait()
    for i in range(parts):
        at = pl.ds(i * n, n)
        for k, dst in enumerate((step_out, moment_out, second_out)):
            reads[k, i].wait()
            if k == 0:
                scaled[at] = held[0, at] * by[0:1, 0:1]
            src = scaled.at[at] if k == 0 else held.at[k, at]
            writes.append(pltpu.make_async_copy(src, dst.at[at], done.at[k, i]))
            writes[-1].start()
    for c in writes:
        c.wait()


def shards(features, label_ids, label_count, weight, moment, second):
    hbm = pl.BlockSpec(memory_space=pltpu.HBM)
    f32, bf16, i32 = jnp.float32, jnp.bfloat16, jnp.int32
    block = jax.ShapeDtypeStruct(weight.shape, f32)
    results = pl.pallas_call(
        kernel,
        name="step",
        out_shape=(block, block, block, jax.ShapeDtypeStruct((8, 128), f32)),
        in_specs=[hbm] * 6,
        out_specs=(hbm, hbm, hbm, hbm),
        scratch_shapes=[
            pltpu.VMEM(features.shape[::-1], bf16),
            pltpu.VMEM(label_ids.shape[::-1], i32),
            pltpu.VMEM((1, BLOCK_Q), i32),
            pltpu.VMEM((4, 8, BLOCK_Q), i32),
            pltpu.VMEM(weight.shape, f32),
            pltpu.VMEM(weight.shape, f32),
            pltpu.VMEM(weight.shape, f32),
            pltpu.VMEM((2, ROWS, HALF), bf16),
            pltpu.VMEM((NZ, NY, NX, 2, BLOCK_D, BLOCK_Q), bf16),
            pltpu.VMEM((9, NY, NX, 8, BLOCK_Q), i32),
            pltpu.VMEM((8, NY, 8, BLOCK_Q), i32),
            pltpu.VMEM((2, ROWS, HALF), f32),
            pltpu.VMEM((28, 2, 128), f32),
            pltpu.VMEM(weight.shape, f32),
            pltpu.VMEM(weight.shape, f32),
            pltpu.VMEM(weight.shape, f32),
            pltpu.VMEM((8, 128), f32),
            pltpu.SemaphoreType.DMA((N_SEMS,)),
            pltpu.SemaphoreType.DMA((N_SEMS,)),
            pltpu.SemaphoreType.DMA((9,)),
        ],
        compiler_params=pltpu.CompilerParams(
            collective_id=0, has_side_effects=True, vmem_limit_bytes=60 << 20
        ),
    )(features.T, label_ids.T, label_count.reshape(1, -1), weight, moment, second)
    return pl.pallas_call(
        finish,
        name="finish",
        out_shape=(block, block, block),
        in_specs=[hbm] * 4,
        out_specs=(hbm, hbm, hbm),
        scratch_shapes=[
            pltpu.VMEM((3, *weight.shape), f32),
            pltpu.VMEM(weight.shape, f32),
            pltpu.VMEM((8, 128), f32),
            pltpu.SemaphoreType.DMA((4, 4)),
            pltpu.SemaphoreType.DMA((3, 4)),
        ],
        compiler_params=pltpu.CompilerParams(vmem_limit_bytes=60 << 20),
    )(*results)


def solution(mesh):
    in_specs = (
        P("dp", "label"),
        P("dp", None),
        P("dp"),
        P(("dp", "label"), None),
        P(("dp", "label"), None),
        P(("dp", "label"), None),
    )
    out_specs = (P(("dp", "label"), None), P(("dp", "label"), None), P(("dp", "label"), None))
    return jax.shard_map(shards, mesh=mesh, in_specs=in_specs, out_specs=out_specs, check_vma=False)
```

time: 72.1 us -> 69.3 us (0.961)
  local copies, waits for them, and re-layouts: 2.07 us -> 0 us
    unnamed x6 -> x0, local copies, waits for them, and re-layouts: 2.07 us -> none
    pallas_call x1, Pallas kernels: 67.7 us -> 65.8 us  [shards(): pl.pallas_call(kernel, name='step', out_shape=(block, block, block, jax.S...]
    pallas_call x1, Pallas kernels: 1.44 us -> 2.71 us  [shards(): pl.pallas_call(finish, name='finish', out_shape=(block, block, block), in...]
where the time goes in v3:
time: 69.3 us; the launch traced here: 69.1 us
  Pallas kernels  68.5 us (99%)
    pallas_call x1, Pallas kernels, shards(): pl.pallas_call(kernel, name='step', out_shape=(block, block, block, jax.S...  65.8 us
    pallas_call x1, Pallas kernels, shards(): pl.pallas_call(finish, name='finish', out_shape=(block, block, block), in...  2.71 us

profile of v3, /device:TPU:1, one launch (start us, length us, event | category | flops | bytes accessed | tf_op | source)
XLA Modules:
  0.0 69.1 jit_solution(16294737353135042818)
XLA Ops:
  0.6 65.8 %step.1 = (f32[256,768]{1,0:T(8,128)}, f32[256,768]{1,0:T(8,128)}, f32[256,768]{1,0:T(8,128)}, f32[8,128]{1,0:T(8,128)}) custom-call(bf16[48,128]{1,0:T(8,128)(2,1)} %bitcast.4, s32[32,128]{1,0:T(8,128)} %bitcast.3, s32[1,128]{1,0:T(1,128)} %bitcast.5, f32[256,768]{1,0:T(8,128)} %weight.1, f32[256,768]{1,0:T(8,128)} %moment.1, f32[256,768]{1,0:T(8,128)} %second.1), custom_call_target="tpu_custom_call" | custom-call | tf_op jit(solution)/shard_map/step/pallas_call | solution.py:395
  66.4 2.7 %finish.1 = (f32[256,768]{1,0:T(8,128)}, f32[256,768]{1,0:T(8,128)}, f32[256,768]{1,0:T(8,128)}) custom-call(f32[256,768]{1,0:T(8,128)} %get-tuple-element.7.update, f32[256,768]{1,0:T(8,128)} %get-tuple-element.8.moment, f32[256,768]{1,0:T(8,128)} %get-tuple-element.9.second, f32[8,128]{1,0:T(8,128)} %get-tuple-element.10.trust), custom_call_target="tpu_custom_call" | custom-call | tf_op jit(solution)/shard_map/finish/pallas_call | solution.py:427

commit v4 on v3

--- a/solution.py
+++ b/solution.py
@@ -27,20 +27,24 @@
     "9": (9, 10, "y"),
 }
 FORWARDED = ()
-LAST = ("5", "11")
-Z_ORDER = (5, 12, 9, 4, 7, 6, 11, 10, 8)
+LAST = ()
 OTHERS = (1, 3, 2)
-Z_FAR_FIRST = (8, 7, 9, 6, 10, 5, 11, 4, 12, 3, 13, 2, 14, 1, 15)
-ROW = ((2, 1), (2, 0), (1, 1), (3, 1), (1, 0), (3, 0), (0, 1))
+NEAR_Z = (4, 12, 3, 13, 2, 14, 1, 15)
+FAR_Z = (8, 7, 9, 6, 10, 5, 11)
+PLANE = sorted(
+    ((i, j, k) for i in range(NX) for j in range(NY) for k in range(2) if i or j or k),
+    key=lambda o: -(min(o[0], NX - o[0]) + min(o[1], NY - o[1]) + o[2]),
+)
 
 ORDER = (
-    ("h1", "own"), ("h2", "own"), ("lab", 0), ("h1", "4"), ("lab", 1), ("h1", "12"), ("h3", "own"),
-    ("h1", "11"), ("h1", "5"), ("h1", "10"), ("h1", "6"), ("h2", "4"), ("h1", "78"), ("h1", "9"),
-    ("fz", 0, 0), ("h2", "12"), ("lab", 2), ("h2", "11"), ("h2", "5"), ("h2", "10"), ("h2", "6"),
-    ("fz", 0, 1), ("fz", 0, 2), ("lab", 3), ("fz", 0, 3), ("fz", 1, 0), ("h2", "9"), ("h2", "78"),
-    ("h3", "4"), ("fz", 1, 1), ("fz", 1, 2), ("h3", "12"), ("fz", 1, 3), ("fz", 2, 0), ("h3", "5"),
-    ("h3", "6"), ("p", 4), ("fz", 2, 1), ("h3", "10"), ("h3", "11"), ("h3", "9"), ("p", 6),
-    ("fz", 2, 2), ("fz", 2, 3), ("p", 2), ("h3", "78"), ("p", 1, 5, 3), ("p", 0, 7),
+    ("h1", "own"), ("h2", "own"), ("lab", 0), ("zh", 4), ("zh", 12), ("h1", "4"), ("h1", "12"),
+    ("fz", 0, 0), ("lab", 1), ("h1", "11"), ("h1", "5"), ("h2", "12"), ("h3", "own"), ("h1", "9"),
+    ("h1", "6"), ("h2", "4"), ("h1", "10"), ("h1", "78"), ("fz", 1, 0), ("h2", "11"), ("greet",), ("lab", 2),
+    ("h2", "9"), ("h2", "6"), ("fz", 0, 1), ("fz", 0, 2), ("fz", 0, 3), ("lab", 3), ("h2", "78"),
+    ("fz", 2, 0), ("h2", "10"), ("h3", "4"), ("h3", "12"), ("h3", "6"), ("fz", 1, 1), ("p", 4),
+    ("fz", 1, 2), ("fz", 1, 3), ("h2", "5"), ("h3", "11"), ("h3", "9"), ("h3", "10"), ("p", 6),
+    ("h3", "78"), ("fz", 2, 1), ("p", 1, 2), ("fz", 2, 2), ("fz", 2, 3), ("h3", "5"),
+    ("p", 0, 7, 3), ("p", 5),
 )
 
 
@@ -66,8 +70,9 @@
             return device(x, y, lax.rem(z + by, NZ), core)
         return device(x, y, z, 1 - core)
 
-    def in_row(by, cores):
-        return device(lax.rem(x + by, NX), y, z, lax.rem(core + cores, 2))
+    def in_plane(offset):
+        i, j, k = offset
+        return device(lax.rem(x + i, NX), lax.rem(y + j, NY), z, lax.rem(core + k, 2))
 
     loads = {}
     for i, (name, src, dst) in enumerate(
@@ -84,12 +89,15 @@
         loads[name].start()
 
     barrier = pltpu.get_barrier_semaphore()
-    column = [along("z", by) for by in Z_FAR_FIRST]
-    file = [along("y", by) for by in (2, 1, 3)]
-    row_ = [in_row(*o) for o in ROW]
-    greeted = column + file + row_
-    for to in greeted:
-        pl.semaphore_signal(barrier, inc=1, device_id=to, device_id_type=MESH)
+    def greet(devices):
+        for to in devices:
+            pl.semaphore_signal(barrier, inc=1, device_id=to, device_id_type=MESH)
+
+    near = [along("z", by) for by in NEAR_Z]
+    near += [in_plane(o) for o in PLANE if sum(1 for i in o if i) == 1]
+    greet(near)
+    later = [along("z", by) for by in FAR_Z]
+    later += [in_plane(o) for o in PLANE if sum(1 for i in o if i) > 1]
 
     loads["features"].wait()
     held[0, y, x, core] = feat_in[...]
@@ -120,7 +128,7 @@
             part, part, send.at[0], sem, device_id=along("z", 1), device_id_type=MESH
         ).wait_recv()
 
-    pl.semaphore_wait(barrier, len(greeted))
+    pl.semaphore_wait(barrier, len(near))
 
     toward = 1 - 2 * core
     label_z = sems()[1]
@@ -136,17 +144,30 @@
         )
 
     z_recv = {name: sems()[1] for name in GROUPS if name != "own"}
-    for d in Z_ORDER:
-        there = NZ - d
-        name = next(n for n, (a, b, _) in GROUPS.items() if a <= there < b)
-        copy(held.at[0, y, x, core], held.at[there, y, x, core], along("z", d), z_recv[name])
+
+    def slot(r):
+        found = [n for n, (a, b, _) in GROUPS.items() if a <= r < b]
+        return found[0] if found else "z" + str(min(r, NZ - r))
+
+    def block(r):
+        return held.at[r, y, x, core]
+
+    for r in (4, 12):
+        copy(block(0), block(r), along("z", NZ - r), z_recv[slot(r)])
+
+    def hand_on(first):
+        arrived(block(first), z_recv[slot(first)])
+        there = (8, 7, 6, 5) if first == 4 else (9, 10, 11)
+        for r in there:
+            by = (NZ + first - r) % NZ
+            copy(block(first), block(r), along("z", by), z_recv[slot(r)])
 
     hops, cross = {}, {}
 
     def hop1(name):
         a, b, axis = GROUPS[name]
         part = held.at[a:b, y, x, core]
-        if name != "own":
+        if name not in ("own", "4", "12"):
             arrived(part, z_recv[name])
         hops[name] = [copy(part, part, along(axis, i)) for i in OTHERS]
 
@@ -223,10 +244,6 @@
             waiting.add(name)
             for c in cross[name]:
                 c.wait_recv()
-
-    def slot(r):
-        found = [n for n, (a, b, _) in GROUPS.items() if a <= r < b]
-        return found[0] if found else "z" + str(min(r, NZ - r))
 
     first = (dp * 16 + lb) * ROWS
 
@@ -278,9 +295,9 @@
         def slab(at):
             return jnp.concatenate([held[at, i].reshape(HALF, BLOCK_Q) for i in range(NY)], axis=1)
 
-        block = jnp.concatenate([slab(r), slab(r + 8)], axis=0)
+        rows = jnp.concatenate([slab(r), slab(r + 8)], axis=0)
         both = jnp.concatenate([w_bf[lo], w_bf[1 - lo]], axis=1)
-        scores = jnp.dot(both, block, preferred_element_type=jnp.float32)
+        scores = jnp.dot(both, rows, preferred_element_type=jnp.float32)
         prob = 1.0 / (1.0 + jnp.exp2(scores * (-SCALE * LOG2_E)))
         marks = jnp.concatenate([words[r, i] for i in range(NY)], axis=1)
         bits = jnp.left_shift(jnp.int32(1), lax.broadcasted_iota(jnp.int32, (32, q), 0))
@@ -289,17 +306,21 @@
         )
         dscore = (prob - jnp.where(target, 1.0, 0.0)).astype(jnp.bfloat16)
         dims = (((1,), (1,)), ((), ()))
-        g = lax.dot_general(dscore, block, dims, preferred_element_type=jnp.float32)
+        g = lax.dot_general(dscore, rows, dims, preferred_element_type=jnp.float32)
         acc[lo] += g[:, :HALF]
         acc[1 - lo] += g[:, HALF:]
 
-    steps = {"h1": hop1, "h2": hop2, "h2b": forward, "h3": hop3, "fz": from_z, "lab": label}
+    steps = {"zh": hand_on, "h1": hop1, "h2": hop2, "h2b": forward, "h3": hop3, "fz": from_z, "lab": label}
     for at, (what, *args) in enumerate(ORDER):
         if at == 2:
             loads["weight"].wait()
             w_bf[0] = w_in[:, :HALF].astype(jnp.bfloat16)
             w_bf[1] = w_in[:, HALF:].astype(jnp.bfloat16)
             acc[...] = jnp.zeros_like(acc)
+        if what == "greet":
+            done("own")
+            greet(later)
+            continue
         if what != "p":
             steps[what](*args)
             continue
@@ -344,10 +365,17 @@
         c.start()
     value = jnp.concatenate([jnp.sum(t, axis=0, keepdims=True) for t in totals], axis=0)
 
-    base = 3
-    for stage, to in enumerate((row_, file, column)):
+    pl.semaphore_wait(barrier, len(later))
+    gathered = list(sent)
+    base = 2
+    column = [along("z", by) for by in (*FAR_Z, *NEAR_Z)]
+    for stage, to in enumerate(([in_plane(o) for o in PLANE], column)):
         sums[stage] = value
         cs = [copy(sums.at[stage], sums.at[base + i], d) for i, d in enumerate(to)]
+        for c in gathered[stage::2]:
+            c.wait_send()
+        for c in stores if stage else ():
+            c.wait()
         for c in cs:
             c.wait_recv()
         value = value + jnp.sum(sums[base : base + len(to)], axis=0)
@@ -357,10 +385,8 @@
     trust_out[...] = jnp.broadcast_to(trust, trust_out.shape)
     store = pltpu.make_async_copy(trust_out, trust_hbm, local.at[0])
     store.start()
-    for c in sent:
+    for c in sent[len(gathered) :]:
         c.wait_send()
-    for c in stores:
-        c.wait()
     store.wait()
 
 
@@ -411,7 +437,7 @@
             pltpu.VMEM((9, NY, NX, 8, BLOCK_Q), i32),
             pltpu.VMEM((8, NY, 8, BLOCK_Q), i32),
             pltpu.VMEM((2, ROWS, HALF), f32),
-            pltpu.VMEM((28, 2, 128), f32),
+            pltpu.VMEM((48, 2, 128), f32),
             pltpu.VMEM(weight.shape, f32),
             pltpu.VMEM(weight.shape, f32),
             pltpu.VMEM(weight.shape, f32),

time: 69.3 us -> 64.4 us (0.929)
  Pallas kernels: 68.5 us -> 63.5 us
    pallas_call x1, Pallas kernels: 65.8 us -> 60.8 us  [shards(): pl.pallas_call(kernel, name='step', out_shape=(block, block, block, jax.S...]
where the time goes in v4:
time: 64.4 us; the launch traced here: 64.2 us
  Pallas kernels  63.5 us (99%)
    pallas_call x1, Pallas kernels, shards(): pl.pallas_call(kernel, name='step', out_shape=(block, block, block, jax.S...  60.8 us
    pallas_call x1, Pallas kernels, shards(): pl.pallas_call(finish, name='finish', out_shape=(block, block, block), in...  2.71 us

profile of v4, /device:TPU:1, one launch (start us, length us, event | category | flops | bytes accessed | tf_op | source)
XLA Modules:
  0.0 64.2 jit_solution(7517952275660416383)
XLA Ops:
  0.6 60.8 %step.1 = (f32[256,768]{1,0:T(8,128)}, f32[256,768]{1,0:T(8,128)}, f32[256,768]{1,0:T(8,128)}, f32[8,128]{1,0:T(8,128)}) custom-call(bf16[48,128]{1,0:T(8,128)(2,1)} %bitcast.4, s32[32,128]{1,0:T(8,128)} %bitcast.3, s32[1,128]{1,0:T(1,128)} %bitcast.5, f32[256,768]{1,0:T(8,128)} %weight.1, f32[256,768]{1,0:T(8,128)} %moment.1, f32[256,768]{1,0:T(8,128)} %second.1), custom_call_target="tpu_custom_call" | custom-call | tf_op jit(solution)/shard_map/step/pallas_call | solution.py:421
  61.5 2.7 %finish.1 = (f32[256,768]{1,0:T(8,128)}, f32[256,768]{1,0:T(8,128)}, f32[256,768]{1,0:T(8,128)}) custom-call(f32[256,768]{1,0:T(8,128)} %get-tuple-element.7.update, f32[256,768]{1,0:T(8,128)} %get-tuple-element.8.moment, f32[256,768]{1,0:T(8,128)} %get-tuple-element.9.second, f32[8,128]{1,0:T(8,128)} %get-tuple-element.10.trust), custom_call_target="tpu_custom_call" | custom-call | tf_op jit(solution)/shard_map/finish/pallas_call | solution.py:453

commit v5 on v4

--- a/solution.py
+++ b/solution.py
@@ -13,7 +13,8 @@
 BLOCK_D, BLOCK_Q = 48, 128
 SCALE = 1.0 / WIDTH**0.5
 LOG2_E = 1.4426950408889634
-N_SEMS = 230
+KINDS = ("label", "z", "hop1", "hop2", "up_down", "core", "plane", "column")
+N_ARRIVALS = 58
 
 GROUPS = {
     "own": (0, 1, "y"),
@@ -26,8 +27,6 @@
     "78": (7, 9, "x"),
     "9": (9, 10, "y"),
 }
-FORWARDED = ()
-LAST = ()
 OTHERS = (1, 3, 2)
 NEAR_Z = (4, 12, 3, 13, 2, 14, 1, 15)
 FAR_Z = (8, 7, 9, 6, 10, 5, 11)
@@ -108,34 +107,34 @@
     row, col = jnp.where(core == 0, y, x), jnp.where(core == 0, x, y)
     labels[3 + 5 * core, row, col] = ids_t[x]
 
-    used_sems, sent = [0], []
-
-    def sems():
-        used_sems[0] += 1
-        return send.at[used_sems[0] - 1], recv.at[used_sems[0] - 1]
-
-    def copy(src, dst, to, recv_sem=None):
-        s, r = sems()
-        c = pltpu.make_async_remote_copy(
-            src, dst, s, r if recv_sem is None else recv_sem, device_id=to, device_id_type=MESH
+    arrivals = {}
+
+    def arrival(key):
+        return recv.at[arrivals.setdefault(key, len(arrivals))]
+
+    def described(src, dst, to, kind, key):
+        return pltpu.make_async_remote_copy(
+            src, dst, send.at[KINDS.index(kind)], arrival(key), device_id=to, device_id_type=MESH
         )
-        sent.append(c)
-        c.start()
-        return c
-
-    def arrived(part, sem):
-        pltpu.make_async_remote_copy(
-            part, part, send.at[0], sem, device_id=along("z", 1), device_id_type=MESH
-        ).wait_recv()
+
+    def copy(src, dst, to, kind, key):
+        described(src, dst, to, kind, key).start()
+
+    def arrived(part, key):
+        described(part, part, along("z", 1), "z", key).wait_recv()
+
+    def blocks(n):
+        if n <= NZ:
+            return held.at[0:n, 0, 0, 0]
+        return held.at[0 : n // 4, :, 0, 0] if n < 64 else held.at[0 : n // 32]
 
     pl.semaphore_wait(barrier, len(near))
 
     toward = 1 - 2 * core
-    label_z = sems()[1]
     for k in (3, 2, 1, 0):
         to = device(x, y, lax.rem(z + toward * (k + 1) + NZ, NZ), core)
         there = 8 - core if k == 3 else (2 - k) * (1 - core) + (4 + k) * core
-        copy(ids_t.at[x], labels.at[there, row, col], to, label_z)
+        copy(ids_t.at[x], labels.at[there, row, col], to, "label", ("label", 0))
 
     def label_hop(first, i):
         on_x = (core == 0) == first
@@ -143,8 +142,6 @@
             jnp.where(on_x, lax.rem(x + i, NX), x), jnp.where(on_x, y, lax.rem(y + i, NY)), z, core
         )
 
-    z_recv = {name: sems()[1] for name in GROUPS if name != "own"}
-
     def slot(r):
         found = [n for n, (a, b, _) in GROUPS.items() if a <= r < b]
         return found[0] if found else "z" + str(min(r, NZ - r))
@@ -153,97 +150,73 @@
         return held.at[r, y, x, core]
 
     for r in (4, 12):
-        copy(block(0), block(r), along("z", NZ - r), z_recv[slot(r)])
+        copy(block(0), block(r), along("z", NZ - r), "z", ("z", slot(r)))
 
     def hand_on(first):
-        arrived(block(first), z_recv[slot(first)])
+        arrived(block(first), ("z", slot(first)))
         there = (8, 7, 6, 5) if first == 4 else (9, 10, 11)
         for r in there:
             by = (NZ + first - r) % NZ
-            copy(block(first), block(r), along("z", by), z_recv[slot(r)])
-
-    hops, cross = {}, {}
+            copy(block(first), block(r), along("z", by), "z", ("z", slot(r)))
+
+    crossing = {}
 
     def hop1(name):
         a, b, axis = GROUPS[name]
         part = held.at[a:b, y, x, core]
         if name not in ("own", "4", "12"):
-            arrived(part, z_recv[name])
-        hops[name] = [copy(part, part, along(axis, i)) for i in OTHERS]
-
-    def line(name, at, part=slice(0, 4)):
-        a, b, axis = GROUPS[name]
-        return held.at[a:b, at, part, core] if axis == "x" else held.at[a:b, part, at, core]
-
-    def to_core(name, part):
-        cross.setdefault(name, []).append(copy(part, part, along("core", 1)))
-
-    passed = [[], [], []]
-
-    def to_z(k, at):
+            arrived(part, ("z", name))
+        for i in OTHERS:
+            copy(part, part, along(axis, i), "hop1", ("hop1", name))
+
+    def to_core(name, part, n):
+        crossing[name] = crossing.get(name, 0) + n
+        copy(part, part, along("core", 1), "core", ("core", name))
+
+    def to_z(k, n, at):
         ups = held.at[(NZ - k) % NZ, :, at, core], held.at[NZ - 1 - k, :, at, core]
         downs = held.at[k, :, at, core], held.at[k + 1, :, at, core]
-        passed[k].append((copy(*ups, along("z", 1)), copy(*downs, along("z", NZ - 1))))
+        copy(*ups, along("z", 1), "up_down", ("up_down", k, n))
+        copy(*downs, along("z", NZ - 1), "up_down", ("up_down", k, n))
 
     def from_z(k, n):
         at = lax.rem(x + 4 - (0, *OTHERS)[n], 4)
-        for c in passed[k][n]:
-            c.wait_recv()
+        arrived(blocks(8), ("up_down", k, n))
         if k < 2:
-            to_z(k + 1, at)
+            to_z(k + 1, n, at)
         for r in (k + 1, NZ - 1 - k):
             if k == 2:
-                to_core("z3", held.at[r, :, at, core])
+                to_core("z3", held.at[r, :, at, core], 4)
             elif n == 3:
-                to_core("z" + str(k + 1), held.at[r, :, :, core])
+                to_core("z" + str(k + 1), held.at[r, :, :, core], 16)
 
     def hop2(name):
-        other, mine = ("y", y) if GROUPS[name][2] == "x" else ("x", x)
-        for c in hops[name]:
-            c.wait_recv()
-        part = line(name, mine)
-        to = OTHERS[:2] if name in FORWARDED else OTHERS
-        hops[name] = [copy(part, part, along(other, i)) for i in to]
+        a, b, axis = GROUPS[name]
+        arrived(blocks(3 * (b - a)), ("hop1", name))
+        part = held.at[a:b, y, :, core] if axis == "x" else held.at[a:b, :, x, core]
+        for n, i in enumerate(OTHERS):
+            key = ("hop2", name, n) if name == "own" else ("hop2", name)
+            copy(part, part, along("y" if axis == "x" else "x", i), "hop2", key)
         if name == "own":
-            to_z(0, mine)
-        if name in LAST:
-            to_core(name, part)
-
-    def forward(name):
-        other, mine = ("y", y) if GROUPS[name][2] == "x" else ("x", x)
-        halves = []
-        for c, i in zip(hops[name], OTHERS[:2], strict=True):
-            c.wait_recv()
-            at = lax.rem(mine + 4 - i, 4)
-            part = line(name, at, slice(0, 2) if i == 1 else slice(2, 4))
-            halves.append(copy(part, part, along(other, i)))
-            if name in LAST:
-                to_core(name, line(name, at))
-        hops[name] = halves
+            to_z(0, 0, x)
 
     def hop3(name):
-        a, b, axis = GROUPS[name]
-        mine = y if axis == "x" else x
-        for c, i in zip(hops[name], OTHERS, strict=False):
-            c.wait_recv()
-            at = lax.rem(mine + 4 - i, 4)
-            if name == "own":
-                to_z(0, at)
-            if name in LAST and name not in FORWARDED:
-                to_core(name, line(name, at))
-        if name not in LAST:
-            for r in range(a, b):
-                to_core(name, held.at[r, :, :, core])
-        elif name in FORWARDED:
-            to_core(name, line(name, lax.rem(mine + 2, 4)))
+        a, b, _ = GROUPS[name]
+        if name == "own":
+            for n, i in enumerate(OTHERS):
+                arrived(blocks(4), ("hop2", name, n))
+                to_z(0, n + 1, lax.rem(x + 4 - i, 4))
+        else:
+            arrived(blocks(12 * (b - a)), ("hop2", name))
+        for r in range(a, b):
+            to_core(name, held.at[r, :, :, core], 16)
 
     waiting = set()
 
     def done(name):
         if name not in waiting:
             waiting.add(name)
-            for c in cross[name]:
-                c.wait_recv()
+            arrived(blocks(crossing[name]), ("core", name))
 
     first = (dp * 16 + lb) * ROWS
 
@@ -267,26 +240,18 @@
         words[pair, at] = out
         return core
 
-    label_sent = []
-
     def label(stage):
-        if stage == 0:
-            arrived(labels.at[0:4, row, col], label_z)
-        for c in label_sent:
-            c.wait_recv()
-        label_sent.clear()
-        if stage == 0:
-            part = labels.at[pl.ds(4 * core, 4), row, col]
-            label_sent.extend(copy(part, part, label_hop(True, i)) for i in OTHERS)
-        elif stage == 1:
-            part = labels.at[pl.ds(4 * core, 4), row]
-            label_sent.extend(copy(part, part, label_hop(False, i)) for i in OTHERS)
-        elif stage == 2:
-            part = labels.at[pl.ds(4 * core, 4)]
-            label_sent.append(copy(part, part, along("core", 1)))
-        else:
+        part = labels.at[0 : (0, 0, 3, 4)[stage]] if stage > 1 else labels.at[0 : 4 - stage, 0]
+        arrived(part if stage else labels.at[0:4, 0, 0], ("label", stage))
+        if stage == 3:
             for i in range(2):
                 lax.fori_loop(0, 4 * NY, lambda n, _, i=i: (mark(n, i), 0)[1], 0)
+            return
+        mine = labels.at[pl.ds(4 * core, 4)]
+        part = (mine.at[:, row, col], mine.at[:, row], mine)[stage]
+        to = [label_hop(stage == 0, i) for i in OTHERS] if stage < 2 else [along("core", 1)]
+        for d in to:
+            copy(part, part, d, "label", ("label", stage + 1))
 
     def pair(r):
         lo = lax.rem(z + r, NZ) // 8
@@ -310,7 +275,7 @@
         acc[lo] += g[:, :HALF]
         acc[1 - lo] += g[:, HALF:]
 
-    steps = {"zh": hand_on, "h1": hop1, "h2": hop2, "h2b": forward, "h3": hop3, "fz": from_z, "lab": label}
+    steps = {"zh": hand_on, "h1": hop1, "h2": hop2, "h3": hop3, "fz": from_z, "lab": label}
     for at, (what, *args) in enumerate(ORDER):
         if at == 2:
             loads["weight"].wait()
@@ -366,18 +331,32 @@
     value = jnp.concatenate([jnp.sum(t, axis=0, keepdims=True) for t in totals], axis=0)
 
     pl.semaphore_wait(barrier, len(later))
-    gathered = list(sent)
     base = 2
     column = [along("z", by) for by in (*FAR_Z, *NEAR_Z)]
+    left = {
+        "label": labels.at[0:8],
+        "z": held.at[0:9, 0, 0, 0],
+        "hop1": held.at[0:15, 0:2, 0, 0],
+        "hop2": held.at[0:15, :, 0:2, 0],
+        "up_down": held.at[0:3],
+        "core": held.at[0:8],
+    }
+
+    def have_left(kind, part):
+        described(part, part, along("z", 1), kind, ("label", 0)).wait_send()
+
     for stage, to in enumerate(([in_plane(o) for o in PLANE], column)):
+        kind = ("plane", "column")[stage]
         sums[stage] = value
-        cs = [copy(sums.at[stage], sums.at[base + i], d) for i, d in enumerate(to)]
-        for c in gathered[stage::2]:
-            c.wait_send()
-        for c in stores if stage else ():
-            c.wait()
-        for c in cs:
-            c.wait_recv()
+        for i, d in enumerate(to):
+            copy(sums.at[stage], sums.at[base + i], d, kind, kind)
+        if stage:
+            for c in stores:
+                c.wait()
+        else:
+            for sent, part in left.items():
+                have_left(sent, part)
+        arrived(sums.at[base : base + len(to)], kind)
         value = value + jnp.sum(sums[base : base + len(to)], axis=0)
         base += len(to)
     norms = jnp.sqrt(jnp.sum(value, axis=1, keepdims=True))
@@ -385,8 +364,8 @@
     trust_out[...] = jnp.broadcast_to(trust, trust_out.shape)
     store = pltpu.make_async_copy(trust_out, trust_hbm, local.at[0])
     store.start()
-    for c in sent[len(gathered) :]:
-        c.wait_send()
+    have_left("plane", sums.at[0 : len(PLANE)])
+    have_left("column", sums.at[0 : len(column)])
     store.wait()
 
 
@@ -442,8 +421,8 @@
             pltpu.VMEM(weight.shape, f32),
             pltpu.VMEM(weight.shape, f32),
             pltpu.VMEM((8, 128), f32),
-            pltpu.SemaphoreType.DMA((N_SEMS,)),
-            pltpu.SemaphoreType.DMA((N_SEMS,)),
+            pltpu.SemaphoreType.DMA((len(KINDS),)),
+            pltpu.SemaphoreType.DMA((N_ARRIVALS,)),
             pltpu.SemaphoreType.DMA((9,)),
         ],
         compiler_params=pltpu.CompilerParams(

time: 64.4 us -> 60.8 us (0.944)
  Pallas kernels: 63.5 us -> 60 us
    pallas_call x1, Pallas kernels: 60.8 us -> 57.3 us  [shards(): pl.pallas_call(kernel, name='step', out_shape=(block, block, block, jax.S...]
where the time goes in v5:
time: 60.8 us; the launch traced here: 60.6 us
  Pallas kernels  60 us (99%)
  between operations  0.64 us (1%)
    pallas_call x1, Pallas kernels, shards(): pl.pallas_call(kernel, name='step', out_shape=(block, block, block, jax.S...  57.3 us
    pallas_call x1, Pallas kernels, shards(): pl.pallas_call(finish, name='finish', out_shape=(block, block, block), in...  2.71 us

profile of v5, /device:TPU:1, one launch (start us, length us, event | category | flops | bytes accessed | tf_op | source)
XLA Modules:
  0.0 60.6 jit_solution(9173202128101906101)
XLA Ops:
  0.6 57.3 %step.1 = (f32[256,768]{1,0:T(8,128)}, f32[256,768]{1,0:T(8,128)}, f32[256,768]{1,0:T(8,128)}, f32[8,128]{1,0:T(8,128)}) custom-call(bf16[48,128]{1,0:T(8,128)(2,1)} %bitcast.4, s32[32,128]{1,0:T(8,128)} %bitcast.3, s32[1,128]{1,0:T(1,128)} %bitcast.5, f32[256,768]{1,0:T(8,128)} %weight.1, f32[256,768]{1,0:T(8,128)} %moment.1, f32[256,768]{1,0:T(8,128)} %second.1), custom_call_target="tpu_custom_call" | custom-call | tf_op jit(solution)/shard_map/step/pallas_call | solution.py:400
  57.9 2.7 %finish.1 = (f32[256,768]{1,0:T(8,128)}, f32[256,768]{1,0:T(8,128)}, f32[256,768]{1,0:T(8,128)}) custom-call(f32[256,768]{1,0:T(8,128)} %get-tuple-element.7.update, f32[256,768]{1,0:T(8,128)} %get-tuple-element.8.moment, f32[256,768]{1,0:T(8,128)} %get-tuple-element.9.second, f32[8,128]{1,0:T(8,128)} %get-tuple-element.10.trust), custom_call_target="tpu_custom_call" | custom-call | tf_op jit(solution)/shard_map/finish/pallas_call | solution.py:432

commit v6 on v5

--- a/solution.py
+++ b/solution.py
@@ -48,10 +48,10 @@
 
 
 def kernel(
-    features, ids, count, weight, moment, second,
-    update_hbm, moment_hbm, second_hbm, trust_hbm,
-    feat_in, ids_in, count_in, ids_t, w_in, mom_in, sec_in, w_bf, held, labels, words, acc, sums,
-    update_out, moment_out, second_out, trust_out, send, recv, local,
+    packed, weight, moment, second,
+    update_out, moment_out, second_out, trust_out,
+    ids_t, w_in, mom_in, sec_in, w_bf, held, labels, words, acc, sums,
+    send, recv, local,
 ):
     dp, lb = lax.axis_index("dp"), lax.axis_index("label")
     x, y, core = lax.rem(lb // 2, NX), lax.rem(dp, NY), lax.rem(lb, 2)
@@ -76,9 +76,6 @@
     loads = {}
     for i, (name, src, dst) in enumerate(
         [
-            ("features", features, feat_in),
-            ("ids", ids, ids_in),
-            ("count", count, count_in),
             ("weight", weight, w_in),
             ("moment", moment, mom_in),
             ("second", second, sec_in),
@@ -98,12 +95,8 @@
     later = [along("z", by) for by in FAR_Z]
     later += [in_plane(o) for o in PLANE if sum(1 for i in o if i) > 1]
 
-    loads["features"].wait()
-    held[0, y, x, core] = feat_in[...]
-    loads["ids"].wait()
-    loads["count"].wait()
-    used = lax.broadcasted_iota(jnp.int32, ids_in.shape, 0) < count_in[...]
-    ids_t[...] = jnp.where(used, ids_in[...], -1).reshape(4, 8, BLOCK_Q)
+    held[0, y, x, core] = packed[:BLOCK_D].astype(jnp.bfloat16)
+    ids_t[...] = packed[BLOCK_D:].astype(jnp.int32).reshape(4, 8, BLOCK_Q)
     row, col = jnp.where(core == 0, y, x), jnp.where(core == 0, x, y)
     labels[3 + 5 * core, row, col] = ids_t[x]
 
@@ -321,13 +314,6 @@
 
     zero = jnp.zeros((8, 128), jnp.float32)
     totals = lax.fori_loop(0, ROWS // step_rows, refresh, (zero, zero))
-    stores = [
-        pltpu.make_async_copy(update_out, update_hbm, local.at[6]),
-        pltpu.make_async_copy(moment_out, moment_hbm, local.at[7]),
-        pltpu.make_async_copy(second_out, second_hbm, local.at[8]),
-    ]
-    for c in stores:
-        c.start()
     value = jnp.concatenate([jnp.sum(t, axis=0, keepdims=True) for t in totals], axis=0)
 
     pl.semaphore_wait(barrier, len(later))
@@ -350,10 +336,7 @@
         sums[stage] = value
         for i, d in enumerate(to):
             copy(sums.at[stage], sums.at[base + i], d, kind, kind)
-        if stage:
-            for c in stores:
-                c.wait()
-        else:
+        if stage == 0:
             for sent, part in left.items():
                 have_left(sent, part)
         arrived(sums.at[base : base + len(to)], kind)
@@ -362,51 +345,42 @@
     norms = jnp.sqrt(jnp.sum(value, axis=1, keepdims=True))
     trust = norms[0:1] / (norms[1:2] + 1e-06)
     trust_out[...] = jnp.broadcast_to(trust, trust_out.shape)
-    store = pltpu.make_async_copy(trust_out, trust_hbm, local.at[0])
-    store.start()
     have_left("plane", sums.at[0 : len(PLANE)])
     have_left("column", sums.at[0 : len(column)])
-    store.wait()
-
-
-def finish(update, moment, second, trust, step_out, moment_out, second_out, held, scaled, by, given, done):
-    parts, n = 4, ROWS // 4
-    factor = pltpu.make_async_copy(trust, by, given.at[3, 0])
-    factor.start()
-    reads, writes = {}, []
-    for i in range(parts):
+
+
+def finish(update, moment, second, trust, step_out, moment_out, second_out, scaled, done):
+    copies = [
+        pltpu.make_async_copy(moment, moment_out, done.at[0]),
+        pltpu.make_async_copy(second, second_out, done.at[1]),
+    ]
+    for c in copies:
+        c.start()
+    n = ROWS // 4
+    for i in range(4):
         at = pl.ds(i * n, n)
-        for k, src in enumerate((update, moment, second)):
-            reads[k, i] = pltpu.make_async_copy(src.at[at], held.at[k, at], given.at[k, i])
-            reads[k, i].start()
-    factor.wait()
-    for i in range(parts):
-        at = pl.ds(i * n, n)
-        for k, dst in enumerate((step_out, moment_out, second_out)):
-            reads[k, i].wait()
-            if k == 0:
-                scaled[at] = held[0, at] * by[0:1, 0:1]
-            src = scaled.at[at] if k == 0 else held.at[k, at]
-            writes.append(pltpu.make_async_copy(src, dst.at[at], done.at[k, i]))
-            writes[-1].start()
-    for c in writes:
+        scaled[at] = update[at] * trust[0:1, 0:1]
+        copies.append(pltpu.make_async_copy(scaled.at[at], step_out.at[at], done.at[2 + i]))
+        copies[-1].start()
+    for c in copies:
         c.wait()
 
 
 def shards(features, label_ids, label_count, weight, moment, second):
     hbm = pl.BlockSpec(memory_space=pltpu.HBM)
+    vmem = pl.BlockSpec(memory_space=pltpu.VMEM)
+    used = lax.broadcasted_iota(jnp.int32, label_ids.shape, 1) < label_count[:, None]
+    ids = jnp.where(used, label_ids, -1)
+    packed = jnp.concatenate([features.T.astype(jnp.float32), ids.T.astype(jnp.float32)], axis=0)
     f32, bf16, i32 = jnp.float32, jnp.bfloat16, jnp.int32
     block = jax.ShapeDtypeStruct(weight.shape, f32)
     results = pl.pallas_call(
         kernel,
         name="step",
         out_shape=(block, block, block, jax.ShapeDtypeStruct((8, 128), f32)),
-        in_specs=[hbm] * 6,
-        out_specs=(hbm, hbm, hbm, hbm),
+        in_specs=[vmem, hbm, hbm, hbm],
+        out_specs=(vmem, vmem, vmem, vmem),
         scratch_shapes=[
-            pltpu.VMEM(features.shape[::-1], bf16),
-            pltpu.VMEM(label_ids.shape[::-1], i32),
-            pltpu.VMEM((1, BLOCK_Q), i32),
             pltpu.VMEM((4, 8, BLOCK_Q), i32),
             pltpu.VMEM(weight.shape, f32),
             pltpu.VMEM(weight.shape, f32),
@@ -417,32 +391,22 @@
             pltpu.VMEM((8, NY, 8, BLOCK_Q), i32),
             pltpu.VMEM((2, ROWS, HALF), f32),
             pltpu.VMEM((48, 2, 128), f32),
-            pltpu.VMEM(weight.shape, f32),
-            pltpu.VMEM(weight.shape, f32),
-            pltpu.VMEM(weight.shape, f32),
-            pltpu.VMEM((8, 128), f32),
             pltpu.SemaphoreType.DMA((len(KINDS),)),
             pltpu.SemaphoreType.DMA((N_ARRIVALS,)),
-            pltpu.SemaphoreType.DMA((9,)),
+            pltpu.SemaphoreType.DMA((3,)),
         ],
         compiler_params=pltpu.CompilerParams(
-            collective_id=0, has_side_effects=True, vmem_limit_bytes=60 << 20
+            collective_id=0, has_side_effects=True, vmem_limit_bytes=411 << 17
         ),
-    )(features.T, label_ids.T, label_count.reshape(1, -1), weight, moment, second)
+    )(packed, weight, moment, second)
     return pl.pallas_call(
         finish,
         name="finish",
         out_shape=(block, block, block),
-        in_specs=[hbm] * 4,
+        in_specs=[vmem] * 4,
         out_specs=(hbm, hbm, hbm),
-        scratch_shapes=[
-            pltpu.VMEM((3, *weight.shape), f32),
-            pltpu.VMEM(weight.shape, f32),
-            pltpu.VMEM((8, 128), f32),
-            pltpu.SemaphoreType.DMA((4, 4)),
-            pltpu.SemaphoreType.DMA((3, 4)),
-        ],
-        compiler_params=pltpu.CompilerParams(vmem_limit_bytes=60 << 20),
+        scratch_shapes=[pltpu.VMEM(weight.shape, f32), pltpu.SemaphoreType.DMA((6,))],
+        compiler_params=pltpu.CompilerParams(vmem_limit_bytes=8 << 20),
     )(*results)
 
 

time: 60.8 us -> 59.6 us (0.980)
  Pallas kernels: 60 us -> 58 us
  other arithmetic: 0 us -> 0.74 us
    pallas_call x1, Pallas kernels: 2.71 us -> 1.44 us  [shards(): pl.pallas_call(finish, name='finish', out_shape=(block, block, block), in...]
    convert_element_type x0 -> x2, other arithmetic: none -> 0.74 us  [the longest x1 0.73 us: shards(): ids.T.astype(jnp.float32)]
    pallas_call x1, Pallas kernels: 57.3 us -> 56.6 us  [shards(): pl.pallas_call(kernel, name='step', out_shape=(block, block, block, jax.S...]
where the time goes in v6:
time: 59.6 us; the launch traced here: 59.4 us
  Pallas kernels  58 us (97%)
  other arithmetic  0.74 us (1%)
  between operations  0.66 us (1%)
    pallas_call x1, Pallas kernels, shards(): pl.pallas_call(kernel, name='step', out_shape=(block, block, block, jax.S...  56.6 us
    pallas_call x1, Pallas kernels, shards(): pl.pallas_call(finish, name='finish', out_shape=(block, block, block), in...  1.44 us

profile of v6, /device:TPU:1, one launch (start us, length us, event | category | flops | bytes accessed | tf_op | source)
XLA Modules:
  0.0 59.4 jit_solution(833988722825181177)
XLA Ops:
  0.6 0.0 copy-start
  0.6 0.7 %convert_bitcast_fusion.1 = f32[32,128]{1,0:T(8,128)S(1)} fusion(s32[128,32]{0,1:T(8,128)} %param.7, s32[128]{0:T(128)} %param.8), kind=kLoop, calls=%fused_computation.2 | loop fusion | flops 12288 | bytes 33280 | tf_op jit(solution)/shard_map/convert_element_type | solution.py:374
  1.4 0.0 copy-done
  1.4 56.6 %step.1 = (f32[256,768]{1,0:T(8,128)S(1)}, f32[256,768]{1,0:T(8,128)S(1)}, f32[256,768]{1,0:T(8,128)S(1)}, f32[8,128]{1,0:T(8,128)S(1)}) custom-call(f32[80,128]{1,0:T(8,128)S(1)} %pad_maximum_fusion.packed, f32[256,768]{1,0:T(8,128)} %weight.1, f32[256,768]{1,0:T(8,128)} %moment.1, f32[256,768]{1,0:T(8,128)} %second.1), custom_call_target="tpu_custom_call" | custom-call | tf_op jit(solution)/shard_map/step/pallas_call | solution.py:377
  58.0 1.4 %finish.1 = (f32[256,768]{1,0:T(8,128)}, f32[256,768]{1,0:T(8,128)}, f32[256,768]{1,0:T(8,128)}) custom-call(f32[256,768]{1,0:T(8,128)S(1)} %get-tuple-element.7.update, f32[256,768]{1,0:T(8,128)S(1)} %get-tuple-element.8.moment, f32[256,768]{1,0:T(8,128)S(1)} %get-tuple-element.9.second, f32[8,128]{1,0:T(8,128)S(1)} %get-tuple-element.10.trust), custom_call_target="tpu_custom_call" | custom-call | tf_op jit(solution)/shard_map/finish/pallas_call | solution.py:402
  (2 shorter events, 0.0 us)
Async XLA Ops:
  0.6 0.7 %copy-start = (bf16[128,48]{0,1:T(8,128)(2,1)S(1)}, bf16[128,48]{0,1:T(8,128)(2,1)}, u32[]{:S(2)}) copy-start(bf16[128,48]{0,1:T(8,128)(2,1)} %param.6) | copy-start | bytes 36868

commit v7 on v6

--- a/solution.py
+++ b/solution.py
@@ -36,14 +36,14 @@
 )
 
 ORDER = (
-    ("h1", "own"), ("h2", "own"), ("lab", 0), ("zh", 4), ("zh", 12), ("h1", "4"), ("h1", "12"),
-    ("fz", 0, 0), ("lab", 1), ("h1", "11"), ("h1", "5"), ("h2", "12"), ("h3", "own"), ("h1", "9"),
-    ("h1", "6"), ("h2", "4"), ("h1", "10"), ("h1", "78"), ("fz", 1, 0), ("h2", "11"), ("greet",), ("lab", 2),
-    ("h2", "9"), ("h2", "6"), ("fz", 0, 1), ("fz", 0, 2), ("fz", 0, 3), ("lab", 3), ("h2", "78"),
-    ("fz", 2, 0), ("h2", "10"), ("h3", "4"), ("h3", "12"), ("h3", "6"), ("fz", 1, 1), ("p", 4),
-    ("fz", 1, 2), ("fz", 1, 3), ("h2", "5"), ("h3", "11"), ("h3", "9"), ("h3", "10"), ("p", 6),
-    ("h3", "78"), ("fz", 2, 1), ("p", 1, 2), ("fz", 2, 2), ("fz", 2, 3), ("h3", "5"),
-    ("p", 0, 7, 3), ("p", 5),
+    ("h1", "own"), ("h2", "own"), ("lab", 0), ("zh", 4), ("zh", 12), ("h1", "12"), ("h1", "4"),
+    ("fz", 0, 0), ("lab", 1), ("h1", "11"), ("h2", "12"), ("h1", "5"), ("h3", "own"), ("h1", "6"),
+    ("h1", "9"), ("h2", "4"), ("h1", "10"), ("h1", "78"), ("fz", 1, 0), ("greet",), ("lab", 2),
+    ("h2", "9"), ("h2", "6"), ("fz", 0, 1), ("lab", 3), ("h2", "78"), ("h3", "4"), ("fz", 0, 2),
+    ("h2", "10"), ("h3", "12"), ("fz", 0, 3), ("fz", 1, 1), ("p", 4), ("h3", "9"), ("h2", "11"),
+    ("h3", "6"), ("fz", 1, 2), ("fz", 1, 3), ("h3", "10"), ("h2", "5"), ("fz", 2, 0), ("p", 1),
+    ("fz", 2, 1), ("h3", "78"), ("p", 2), ("h3", "11"), ("p", 6), ("fz", 2, 2), ("fz", 2, 3),
+    ("p", 7), ("h3", "5"), ("p", 0, 3, 5),
 )
 
 

time: 59.6 us -> 59.3 us (level)
  no operation moved by 1% of the time
where the time goes in v7:
time: 59.3 us; the launch traced here: 59.2 us
  Pallas kernels  57.8 us (97%)
  other arithmetic  0.74 us (1%)
  between operations  0.66 us (1%)
    pallas_call x1, Pallas kernels, shards(): pl.pallas_call(kernel, name='step', out_shape=(block, block, block, jax.S...  56.3 us
    pallas_call x1, Pallas kernels, shards(): pl.pallas_call(finish, name='finish', out_shape=(block, block, block), in...  1.44 us

profile of v7, /device:TPU:1, one launch (start us, length us, event | category | flops | bytes accessed | tf_op | source)
XLA Modules:
  0.0 59.2 jit_solution(2854868558371898642)
XLA Ops:
  0.6 0.0 copy-start
  0.6 0.7 %convert_bitcast_fusion.1 = f32[32,128]{1,0:T(8,128)S(1)} fusion(s32[128,32]{0,1:T(8,128)} %param.7, s32[128]{0:T(128)} %param.8), kind=kLoop, calls=%fused_computation.2 | loop fusion | flops 12288 | bytes 33280 | tf_op jit(solution)/shard_map/convert_element_type | solution.py:374
  1.4 0.0 copy-done
  1.4 56.3 %step.1 = (f32[256,768]{1,0:T(8,128)S(1)}, f32[256,768]{1,0:T(8,128)S(1)}, f32[256,768]{1,0:T(8,128)S(1)}, f32[8,128]{1,0:T(8,128)S(1)}) custom-call(f32[80,128]{1,0:T(8,128)S(1)} %pad_maximum_fusion.packed, f32[256,768]{1,0:T(8,128)} %weight.1, f32[256,768]{1,0:T(8,128)} %moment.1, f32[256,768]{1,0:T(8,128)} %second.1), custom_call_target="tpu_custom_call" | custom-call | tf_op jit(solution)/shard_map/step/pallas_call | solution.py:377
  57.7 1.4 %finish.1 = (f32[256,768]{1,0:T(8,128)}, f32[256,768]{1,0:T(8,128)}, f32[256,768]{1,0:T(8,128)}) custom-call(f32[256,768]{1,0:T(8,128)S(1)} %get-tuple-element.7.update, f32[256,768]{1,0:T(8,128)S(1)} %get-tuple-element.8.moment, f32[256,768]{1,0:T(8,128)S(1)} %get-tuple-element.9.second, f32[8,128]{1,0:T(8,128)S(1)} %get-tuple-element.10.trust), custom_call_target="tpu_custom_call" | custom-call | tf_op jit(solution)/shard_map/finish/pallas_call | solution.py:402
  (2 shorter events, 0.0 us)
Async XLA Ops:
  0.6 0.7 %copy-start = (bf16[128,48]{0,1:T(8,128)(2,1)S(1)}, bf16[128,48]{0,1:T(8,128)(2,1)}, u32[]{:S(2)}) copy-start(bf16[128,48]{0,1:T(8,128)(2,1)} %param.6) | copy-start | bytes 36868

commit v8 on v6

--- a/solution.py
+++ b/solution.py
@@ -123,27 +123,27 @@
 
     pl.semaphore_wait(barrier, len(near))
 
+    def label_hop(first, i):
+        on_x = (core == 0) == first
+        return device(
+            jnp.where(on_x, lax.rem(x + i, NX), x), jnp.where(on_x, y, lax.rem(y + i, NY)), z, core
+        )
+
+    def slot(r):
+        found = [n for n, (a, b, _) in GROUPS.items() if a <= r < b]
+        return found[0] if found else "z" + str(min(r, NZ - r))
+
+    def block(r):
+        return held.at[r, y, x, core]
+
+    for r in (4, 12):
+        copy(block(0), block(r), along("z", NZ - r), "z", ("z", slot(r)))
+
     toward = 1 - 2 * core
     for k in (3, 2, 1, 0):
         to = device(x, y, lax.rem(z + toward * (k + 1) + NZ, NZ), core)
         there = 8 - core if k == 3 else (2 - k) * (1 - core) + (4 + k) * core
         copy(ids_t.at[x], labels.at[there, row, col], to, "label", ("label", 0))
-
-    def label_hop(first, i):
-        on_x = (core == 0) == first
-        return device(
-            jnp.where(on_x, lax.rem(x + i, NX), x), jnp.where(on_x, y, lax.rem(y + i, NY)), z, core
-        )
-
-    def slot(r):
-        found = [n for n, (a, b, _) in GROUPS.items() if a <= r < b]
-        return found[0] if found else "z" + str(min(r, NZ - r))
-
-    def block(r):
-        return held.at[r, y, x, core]
-
-    for r in (4, 12):
-        copy(block(0), block(r), along("z", NZ - r), "z", ("z", slot(r)))
 
     def hand_on(first):
         arrived(block(first), ("z", slot(first)))

time: 59.6 us -> 59.6 us (level)
  no operation moved by 1% of the time
where the time goes in v8:
time: 59.6 us; the launch traced here: 59.4 us
  Pallas kernels  58 us (97%)
  other arithmetic  0.74 us (1%)
  between operations  0.66 us (1%)
    pallas_call x1, Pallas kernels, shards(): pl.pallas_call(kernel, name='step', out_shape=(block, block, block, jax.S...  56.5 us
    pallas_call x1, Pallas kernels, shards(): pl.pallas_call(finish, name='finish', out_shape=(block, block, block), in...  1.44 us

profile of v8, /device:TPU:1, one launch (start us, length us, event | category | flops | bytes accessed | tf_op | source)
XLA Modules:
  0.0 59.4 jit_solution(965602384591599265)
XLA Ops:
  0.6 0.0 copy-start
  0.6 0.7 %convert_bitcast_fusion.1 = f32[32,128]{1,0:T(8,128)S(1)} fusion(s32[128,32]{0,1:T(8,128)} %param.7, s32[128]{0:T(128)} %param.8), kind=kLoop, calls=%fused_computation.2 | loop fusion | flops 12288 | bytes 33280 | tf_op jit(solution)/shard_map/convert_element_type | solution.py:374
  1.4 0.0 copy-done
  1.4 56.5 %step.1 = (f32[256,768]{1,0:T(8,128)S(1)}, f32[256,768]{1,0:T(8,128)S(1)}, f32[256,768]{1,0:T(8,128)S(1)}, f32[8,128]{1,0:T(8,128)S(1)}) custom-call(f32[80,128]{1,0:T(8,128)S(1)} %pad_maximum_fusion.packed, f32[256,768]{1,0:T(8,128)} %weight.1, f32[256,768]{1,0:T(8,128)} %moment.1, f32[256,768]{1,0:T(8,128)} %second.1), custom_call_target="tpu_custom_call" | custom-call | tf_op jit(solution)/shard_map/step/pallas_call | solution.py:377
  57.9 1.4 %finish.1 = (f32[256,768]{1,0:T(8,128)}, f32[256,768]{1,0:T(8,128)}, f32[256,768]{1,0:T(8,128)}) custom-call(f32[256,768]{1,0:T(8,128)S(1)} %get-tuple-element.7.update, f32[256,768]{1,0:T(8,128)S(1)} %get-tuple-element.8.moment, f32[256,768]{1,0:T(8,128)S(1)} %get-tuple-element.9.second, f32[8,128]{1,0:T(8,128)S(1)} %get-tuple-element.10.trust), custom_call_target="tpu_custom_call" | custom-call | tf_op jit(solution)/shard_map/finish/pallas_call | solution.py:402
  (2 shorter events, 0.0 us)
Async XLA Ops:
  0.6 0.7 %copy-start = (bf16[128,48]{0,1:T(8,128)(2,1)S(1)}, bf16[128,48]{0,1:T(8,128)(2,1)}, u32[]{:S(2)}) copy-start(bf16[128,48]{0,1:T(8,128)(2,1)} %param.6) | copy-start | bytes 36868
